TPU v7x, 32 devices: a whole 2x2x4 slice. The times are simulated.
32 devices in a mesh: groups: 2 (over y), row: 4 (over z), col: 2 (over core), chan: 2 (over x).
Axes of the slice: x: 2, y: 2, z: 4, core: 2. Of those that a mesh axis runs over, the one named last changes fastest.
Arguments:
- pair: bfloat16 [48, 24, 128], P(('groups', 'row'), 'col', 'chan'), parts along dimension 0, may hold values from -6 to 6
- token_mask: int32 [48], P('groups'), parts along dimension 0, may hold values 0 or 1
- w_in: bfloat16 [128, 4, 128], P(None, None, 'chan'), may hold values from -0.5 to 0.5
- w_gate: bfloat16 [128, 128], P(None, 'chan'), may hold values from -0.5 to 0.5
- w_out: bfloat16 [128, 128], P('chan'), may hold values from -0.5 to 0.5
- cotangent: bfloat16 [48, 24, 128], P(('groups', 'row'), 'col', 'chan'), parts along dimension 0, may hold values from -6 to 6
Outputs:
- update: bfloat16 [48, 24, 128], P(('groups', 'row'), 'col', 'chan'), parts along dimension 0
- pair_grad: bfloat16 [48, 24, 128], P(('groups', 'row'), 'col', 'chan'), parts along dimension 0
There are 2 independent parts, one for each index of `groups`. A program takes and returns all parts, laid end to end along the dimension named above; an argument that names none is the same for every part. Nothing has to cross between parts.
Inputs may be any that keep to these rules, and one draw needn't show every extreme that they name: `token_mask`: 1 marks a real token, 0 padding.
All inputs are finite; a program needn't handle non-finite values.
Results may differ from a plain program's by a relative error of at most 0.008.
Values may be sent and summed in bfloat16 or wider, within the bound.
A program may use at most 64 MiB of HBM per device.

v0:
```python
import jax
import jax.numpy as jnp
from jax import lax
from jax.sharding import PartitionSpec as P

EPS = 1e-05


def body(pair, token_mask, w_in, w_gate, w_out, cotangent):
    f32 = jnp.float32
    brain_float_half = jnp.bfloat16
    rows = pair.shape[0]
    cols = pair.shape[1]
    chans = pair.shape[2]
    width_c = w_in.shape[0]
    hidden_dev = w_in.shape[2]
    hidden_channel_width = hidden_dev * lax.axis_size("chan")
    row_start = lax.axis_index("row") * rows
    col_start = lax.axis_index("col") * cols
    chan_start = lax.axis_index("chan") * chans
    zfull = lax.all_gather(pair, "chan", axis=2, tiled=True).astype(f32)
    mean_z = jnp.sum(zfull, axis=-1, keepdims=True) / width_c
    square_z = jnp.sum(zfull * zfull, axis=-1, keepdims=True) / width_c
    rstd_z = lax.rsqrt(square_z - mean_z * mean_z + EPS)
    zhat = (zfull - mean_z) * rstd_z
    zn_b = zhat.astype(brain_float_half)
    proj = jnp.einsum("rkc,cqh->rkqh", zn_b, w_in, preferred_element_type=f32)
    maskf = token_mask.astype(f32)
    mask_rows = lax.dynamic_slice_in_dim(maskf, row_start, rows)
    mask_cols = lax.dynamic_slice_in_dim(maskf, col_start, cols)
    pmask = (mask_rows[:, None] * mask_cols[None, :])[..., None]
    sig_one = jax.nn.sigmoid(proj[:, :, 1])
    sig_three = jax.nn.sigmoid(proj[:, :, 3])
    left = (pmask * sig_one * proj[:, :, 0]).astype(brain_float_half)
    right = (pmask * sig_three * proj[:, :, 2]).astype(brain_float_half)
    partial_tri = jnp.einsum(
        "ikh,jkh->ijh",
        left,
        lax.all_gather(right, "row", axis=0, tiled=True),
        preferred_element_type=f32,
    )
    triangle_product = lax.psum_scatter(partial_tri, "col", scatter_dimension=1, tiled=True)
    sum_x, square_x = lax.psum(
        (jnp.sum(triangle_product, axis=-1), jnp.sum(triangle_product * triangle_product, axis=-1)),
        "chan",
    )
    input_mean = (sum_x / hidden_channel_width)[..., None]
    input_inverse_deviation = lax.rsqrt(
        square_x[..., None] / hidden_channel_width - input_mean * input_mean + EPS
    )
    centered_input = (triangle_product - input_mean) * input_inverse_deviation
    normed_input_low_precision = centered_input.astype(brain_float_half)
    out_term = jnp.einsum(
        "rch,hd->rcd", normed_input_low_precision, w_out, preferred_element_type=f32
    )
    proj_out = lax.psum_scatter(out_term, "chan", scatter_dimension=2, tiled=True)
    gate = jax.nn.sigmoid(jnp.einsum("rcd,de->rce", zn_b, w_gate, preferred_element_type=f32))
    update = (gate * proj_out).astype(brain_float_half)
    cot = cotangent.astype(f32)
    dproj = (cot * gate).astype(brain_float_half)
    dgate = (cot * proj_out * gate * (1.0 - gate)).astype(brain_float_half)
    dproj_all = lax.all_gather(dproj, "chan", axis=2, tiled=True)
    normed_input_gradient = jnp.einsum("rcd,hd->rch", dproj_all, w_out, preferred_element_type=f32)
    first_operand, second_operand = lax.psum(
        (
            jnp.sum(normed_input_gradient, axis=-1),
            jnp.sum(normed_input_gradient * centered_input, axis=-1),
        ),
        "chan",
    )
    triangle_gradient = (
        (
            normed_input_gradient
            - (first_operand / hidden_channel_width)[..., None]
            - centered_input * (second_operand / hidden_channel_width)[..., None]
        )
        * input_inverse_deviation
    ).astype(brain_float_half)
    dtri_rows = lax.all_gather(triangle_gradient, "col", axis=1, tiled=True)
    block = dtri_rows
    dleft = jnp.einsum(
        "ijh,jkh->ikh",
        block,
        lax.all_gather(right, "row", axis=0, tiled=True),
        preferred_element_type=f32,
    )
    dtri_turned = lax.all_to_all(dtri_rows, "row", split_axis=1, concat_axis=0, tiled=True)
    block = dtri_turned
    dright = jnp.einsum(
        "ijh,ikh->jkh",
        block,
        lax.all_gather(left, "row", axis=0, tiled=True),
        preferred_element_type=f32,
    )
    dpre = jnp.stack(
        [
            dleft * pmask * sig_one,
            dleft * pmask * proj[:, :, 0] * sig_one * (1.0 - sig_one),
            dright * pmask * sig_three,
            dright * pmask * proj[:, :, 2] * sig_three * (1.0 - sig_three),
        ],
        axis=2,
    ).astype(brain_float_half)
    dzn_term = jnp.einsum("rkqh,cqh->rkc", dpre, w_in, preferred_element_type=f32)
    dzn_term = dzn_term + jnp.einsum("rkd,cd->rkc", dgate, w_gate, preferred_element_type=f32)
    dzn = lax.psum_scatter(dzn_term, "chan", scatter_dimension=2, tiled=True)
    zhat_own = lax.dynamic_slice_in_dim(zhat, chan_start, chans, 2)
    first_z, second_z = lax.psum((jnp.sum(dzn, axis=-1), jnp.sum(dzn * zhat_own, axis=-1)), "chan")
    pair_grad = (
        (dzn - (first_z / width_c)[..., None] - zhat_own * (second_z / width_c)[..., None]) * rstd_z
    ).astype(brain_float_half)
    return (update, pair_grad)


def solution(mesh):
    return jax.shard_map(
        body,
        mesh=mesh,
        in_specs=(
            P(("groups", "row"), "col", "chan"),
            P("groups"),
            P(None, None, "chan"),
            P(None, "chan"),
            P("chan", None),
            P(("groups", "row"), "col", "chan"),
        ),
        out_specs=(P(("groups", "row"), "col", "chan"), P(("groups", "row"), "col", "chan")),
        check_vma=False,
    )
```

profile of v0, /device:TPU:0, one launch (start us, length us, event | category | flops | bytes accessed | tf_op | source)
XLA Modules:
  0.0 112.8 jit_solution(9006108392328280601)
XLA Ops:
  7.2 0.0 reduce-scatter.8.cloned.1.call-start
  7.2 0.7 copy-done.2
  7.9 0.2 copy.126
  8.1 7.1 %all_gather.16 = bf16[6,12,128]{1,0,2:T(8,128)(2,1)S(1)} all-gather(bf16[6,12,64]{1,0,2:T(8,128)(2,1)S(1)} %copy.126), channel_id=1, replica_groups=mesh['groups'=2,'row'=4,'col'=2,'chan'=2] {'chan'}, dimensions={2}, use_global_device_ids=true | all-gather | bytes 27648 | tf_op jit(solution)/shard_map/all_gather | solution.py:21
  15.2 0.2 copy.127
  15.4 0.1 convert_reduce_fusion
  15.5 0.6 copy-done.6
  16.1 0.1 dynamic_slice.10
  16.1 0.1 dynamic_slice.9
  16.2 0.1 broadcast_multiply_fusion
  16.3 0.2 fusion.13
  16.5 0.1 multiply_convert_fusion.7
  16.6 13.8 %all_gather.17 = bf16[24,12,64]{2,1,0:T(8,128)(2,1)S(1)} all-gather(bf16[6,12,64]{2,1,0:T(8,128)(2,1)S(1)} %get-tuple-element.27), channel_id=1, replica_groups=mesh['groups'=2,'row'=4,'col'=2,'chan'=2] {'row'}, dimensions={0}, use_global_device_ids=true | all-gather | bytes 46080 | tf_op jit(solution)/shard_map/all_gather | solution.py:39
  30.5 0.3 copy.134
  30.8 0.2 copy.135
  30.9 0.3 convolution_bitcast_fusion
  31.2 0.8 copy.136
  32.0 0.0 reduce-scatter.8.cloned.1.call-update
  32.0 0.0 reduce-scatter.10.cloned.1.call-start
  32.1 8.6 %reduce-scatter.8.cloned.1.call-done = f32[6,12,64]{2,0,1:T(8,128)} async-done(((f32[6,24,64]{2,0,1:T(8,128)}), f32[6,12,64]{2,0,1:T(8,128)}) %reduce-scatter.8.cloned.1.call-update) | async-done | bytes 18448 | tf_op jit(solution)/shard_map/reduce_scatter | solution.py:42
  40.7 1.0 fusion.53
  41.6 0.1 copy.139
  41.7 0.1 copy.137
  41.8 5.1 %all-reduce.2 = (f32[6,12]{1,0:T(8,128)S(1)}, f32[6,12]{1,0:T(8,128)S(1)}) all-reduce(f32[6,12]{1,0:T(8,128)S(1)} %copy.139, f32[6,12]{1,0:T(8,128)S(1)} %copy.137), channel_id=1, replica_groups=mesh['groups'=2,'row'=4,'col'=2,'chan'=2] {'chan'}, use_global_device_ids=true, to_apply=%region_6.0 | all-reduce | flops 144 | bytes 1152 | tf_op jit(solution)/shard_map/psum | solution.py:43
  46.9 0.2 fusion.31
  47.1 0.3 copy.156
  47.4 0.8 reshape.77
  48.2 13.6 %all_gather.20 = bf16[24,12,64]{2,1,0:T(8,128)(2,1)S(1)} all-gather(bf16[6,12,64]{2,1,0:T(8,128)(2,1)S(1)} %get-tuple-element.26), channel_id=1, replica_groups=mesh['groups'=2,'row'=4,'col'=2,'chan'=2] {'row'}, dimensions={0}, use_global_device_ids=true | all-gather | bytes 46080 | tf_op jit(solution)/shard_map/all_gather | solution.py:92
  61.8 0.3 copy.148
  62.1 0.0 reduce-scatter.10.cloned.1.call-done
  62.2 0.9 reshape.78
  63.0 0.1 copy.157
  63.2 0.6 copy-done.3
  63.8 0.8 fusion.15
  64.6 0.2 copy.140
  64.8 5.7 %all_gather.18 = bf16[6,12,128]{1,0,2:T(8,128)(2,1)S(1)} all-gather(bf16[6,12,64]{1,0,2:T(8,128)(2,1)S(1)} %copy.140), channel_id=1, replica_groups=mesh['groups'=2,'row'=4,'col'=2,'chan'=2] {'chan'}, dimensions={2}, use_global_device_ids=true | all-gather | bytes 27648 | tf_op jit(solution)/shard_map/all_gather | solution.py:62
  70.5 0.3 fusion.52
  70.8 5.0 %all-reduce.1 = (f32[6,12]{1,0:T(8,128)S(1)}, f32[6,12]{1,0:T(8,128)S(1)}) all-reduce(f32[6,12]{1,0:T(8,128)S(1)} %get-tuple-element.9, f32[6,12]{1,0:T(8,128)S(1)} %get-tuple-element.8), channel_id=1, replica_groups=mesh['groups'=2,'row'=4,'col'=2,'chan'=2] {'chan'}, use_global_device_ids=true, to_apply=%region_11.0 | all-reduce | flops 144 | bytes 1152 | tf_op jit(solution)/shard_map/psum | solution.py:64
  75.8 0.1 multiply_convert_fusion.5
  76.0 1.8 %all_gather.19 = bf16[6,24,64]{2,0,1:T(8,128)(2,1)S(1)} all-gather(bf16[6,12,64]{2,0,1:T(8,128)(2,1)S(1)} %copy.142), channel_id=1, replica_groups=mesh['groups'=2,'row'=4,'col'=2,'chan'=2] {'col'}, dimensions={1}, use_global_device_ids=true | all-gather | bytes 27648 | tf_op jit(solution)/shard_map/all_gather | solution.py:79
  77.8 0.1 copy.144
  78.0 0.7 reshape.81
  78.7 4.5 %all-to-all-start = ((bf16[4,2,1152]{2,1,0:T(2,128)(2,1)}), bf16[4,2,1152]{2,1,0:T(2,128)(2,1)S(1)}, u32[]{:S(2)}, u32[]{:S(2)}) async-start(bf16[4,2,1152]{2,1,0:T(2,128)(2,1)} %reshape.81), calls=%async_computation.1 | async-start | bytes 36864 | tf_op jit(solution)/shard_map/all_to_all | solution.py:87
  83.2 0.2 fusion.54
  83.4 0.1 copy.145
  83.5 5.2 %all-to-all-done = bf16[4,2,1152]{2,1,0:T(2,128)(2,1)S(1)} async-done(((bf16[4,2,1152]{2,1,0:T(2,128)(2,1)}), bf16[4,2,1152]{2,1,0:T(2,128)(2,1)S(1)}, u32[]{:S(2)}, u32[]{:S(2)}) %all-to-all-start) | async-done | bytes 18464 | tf_op jit(solution)/shard_map/all_to_all | solution.py:87
  88.8 0.1 reshape.82
  88.9 0.1 copy.149
  89.1 0.2 fusion.55
  89.3 0.1 copy.150
  89.5 0.1 fusion.33
  89.6 0.2 convolution_bitcast_fusion.1
  89.8 0.1 convolution_add_fusion
  89.9 0.3 copy.158
  90.2 0.8 reshape.79
  91.0 0.0 reduce-scatter.12.cloned.1.call-update
  91.0 0.1 fusion.19
  91.1 8.2 %reduce-scatter.12.cloned.1.call-done = f32[64,72]{1,0:T(8,128)} async-done(((f32[128,72]{1,0:T(8,128)}), f32[64,72]{1,0:T(8,128)}) %reduce-scatter.12.cloned.1.call-update) | async-done | bytes 18448
  99.3 0.9 reshape.80
  100.1 0.1 bitcast_reduce_fusion
  100.2 0.1 copy.159
  100.3 0.2 multiply_reduce_fusion
  100.5 5.0 %all-reduce = (f32[6,12]{1,0:T(8,128)S(1)}, f32[6,12]{1,0:T(8,128)S(1)}) all-reduce(f32[6,12]{1,0:T(8,128)S(1)} %multiply_reduce_fusion, f32[6,12]{1,0:T(8,128)S(1)} %bitcast_reduce_fusion), channel_id=1, replica_groups=mesh['groups'=2,'row'=4,'col'=2,'chan'=2] {'chan'}, use_global_device_ids=true, to_apply=%region_16.0 | all-reduce | flops 144 | bytes 1152 | tf_op jit(solution)/shard_map/psum | solution.py:108
  105.5 0.7 multiply_convert_fusion
  (22 shorter events, 0.1 us)
Async XLA Ops:
  7.2 9.1 %copy-start = (bf16[128,4,64]{0,2,1:T(8,128)(2,1)S(1)}, bf16[128,4,64]{0,2,1:T(8,128)(2,1)}, u32[]{:S(2)}) copy-start(bf16[128,4,64]{0,2,1:T(8,128)(2,1)} %param.8) | copy-start | bytes 196612
  7.2 0.8 copy-start.2
  7.2 33.5 %reduce-scatter.8.cloned.1.call-start = ((), (), s32[]{:S(2)}) async-start(), calls=%async_computation.4 | async-start | bytes 147456 | tf_op jit(solution)/shard_map/reduce_scatter | solution.py:42
  15.4 0.7 copy-start.6
  32.0 30.1 %reduce-scatter.10.cloned.1.call-start = ((), (), s32[]{:S(2)}) async-start(), calls=%async_computation.5 | async-start | bytes 98304
  40.6 6.3 %copy-start.1 = (f32[6,12,64]{2,0,1:T(8,128)S(1)}, f32[6,12,64]{2,0,1:T(8,128)}, u32[]{:S(2)}) copy-start(f32[6,12,64]{2,0,1:T(8,128)} %reduce-scatter.8.cloned.1.call-done) | copy-start | bytes 55300
  41.8 5.1 %copy-start.5 = (bf16[64,128]{1,0:T(8,128)(2,1)S(1)}, bf16[64,128]{1,0:T(8,128)(2,1)}, u32[]{:S(2)}) copy-start(bf16[64,128]{1,0:T(8,128)(2,1)} %param.10) | copy-start | bytes 49156
  63.0 0.7 copy-start.3
  63.0 0.7 copy-start.4
  78.7 10.1 %all-to-all-start = ((bf16[4,2,1152]{2,1,0:T(2,128)(2,1)}), bf16[4,2,1152]{2,1,0:T(2,128)(2,1)S(1)}, u32[]{:S(2)}, u32[]{:S(2)}) async-start(bf16[4,2,1152]{2,1,0:T(2,128)(2,1)} %reshape.81), calls=%async_computation.1 | async-start | bytes 36864 | tf_op jit(solution)/shard_map/all_to_all | solution.py:87
  83.2 16.1 %reduce-scatter.12.cloned.1.call-start = ((), (), s32[]{:S(2)}) async-start(), calls=%async_computation.6 | async-start | bytes 98304
Sparse Core Ops, SparseCore 0:
  32.2 8.4 reduce-scatter.7
  48.3 11.0 reduce-scatter.9
  91.1 8.1 reduce-scatter.11
where the time goes:
time: 113 us
  blocking collectives  57.2 us (51%)
  waiting for transfers between devices  22.1 us (20%)
  between operations  14 us (12%)
  local copies, waits for them, and re-layouts  9.73 us (9%)
  starting transfers between devices  4.58 us (4%)
  matrix products  2.66 us (2%)
  other arithmetic  2.55 us (2%)
    all_gather x1, blocking collectives, body(): lax.all_gather(right, 'row', axis=0, tiled=True)  13.8 us
    all_gather x1, blocking collectives, body(): lax.all_gather(left, 'row', axis=0, tiled=True)  13.6 us
    reduce_scatter x1, waiting for transfers between devices, body(): lax.psum_scatter(partial_tri, 'col', scatter_dimension=1, tiled=True)  8.56 us
    unnamed x5, waiting for transfers between devices  8.25 us
    all_gather x1, blocking collectives, body(): zfull = lax.all_gather(pair, 'chan', axis=2, tiled=True).astype(f32)  7.09 us
    unnamed x25, local copies, waits for them, and re-layouts  6.89 us
    all_gather x1, blocking collectives, body(): dproj_all = lax.all_gather(dproj, 'chan', axis=2, tiled=True)  5.73 us
    all_to_all x1, waiting for transfers between devices, body(): lax.all_to_all(dtri_rows, 'row', split_axis=1, concat_axis=0, tiled=True)  5.24 us
  transfers between devices with their start and end apart: 4, of which 3 were waited for; matrix products, arithmetic and copies ran while one was open for 1% of the time, Pallas kernels for 0%

commit v1 on v0

--- a/solution.py
+++ b/solution.py
@@ -1,9 +1,299 @@
+import functools
+
 import jax
 import jax.numpy as jnp
 from jax import lax
+from jax.experimental import pallas as pl
+from jax.experimental.pallas import tpu as pltpu
 from jax.sharding import PartitionSpec as P
 
 EPS = 1e-05
+MESH = pl.DeviceIdType.MESH
+
+
+def sigmoid(x):
+    return 1.0 / (1.0 + jnp.exp(-x))
+
+
+def lane_mean(x):
+    return jnp.sum(x, axis=-1, keepdims=True) * (1.0 / x.shape[-1])
+
+
+def norm_stats(x):
+    mean = lane_mean(x)
+    return mean, lax.rsqrt(lane_mean(x * x) - mean * mean + EPS)
+
+
+def merge(first, second):
+    first, second = first.astype(jnp.float32), second.astype(jnp.float32)
+    axis = first.ndim - 1
+    width = first.shape[-1]
+    low = lax.broadcasted_iota(jnp.int32, first.shape, axis) < width // 2
+    return (
+        jnp.where(low, first, pltpu.roll(second, width // 2, axis)),
+        jnp.where(low, pltpu.roll(first, width // 2, axis), second),
+    )
+
+
+def dot(a, b, transposed=False):
+    return lax.dot_general(
+        a, b, (((1,), (1 if transposed else 0,)), ((), ())), preferred_element_type=jnp.float32
+    )
+
+
+def kernel(
+    n_row, pair_ref, mask_ref, w_in_ref, w_gate_ref, w_out_ref, cot_ref, update_ref, grad_ref,
+    pbuf, cbuf, wbuf, z_s, zh_s, c_s, l_s, r_s, mj_s, u_s, dg_s, da_s, db_s,
+    p_send, p_fwd, p_recv, c_send, c_fwd, c_recv, w_send, w_recv,
+):
+    f32, bf16 = jnp.float32, jnp.bfloat16
+    rows, cols, _ = pair_ref.shape
+    n = rows * n_row
+    width = 2 * pair_ref.shape[2]
+    half_rows = rows // 2
+    pad = pbuf.shape[4]
+    block = rows * n
+    r, c, h = lax.axis_index("row"), lax.axis_index("col"), lax.axis_index("chan")
+    other_c, other_h = 1 - c, 1 - h
+
+    def place(dr, dh):
+        return lax.rem(r + dr, n_row), lax.rem(h + dh, 2)
+
+    steps = [(dr, dh) for dr in range(n_row) for dh in range(2)]
+    far = [s for s in steps if s != (0, 0)]
+
+    barrier = pltpu.get_barrier_semaphore()
+    for dr, dh in far:
+        pr, ph = place(dr, dh)
+        pl.semaphore_signal(barrier, inc=1, device_id={"row": pr, "chan": ph}, device_id_type=MESH)
+    pl.semaphore_signal(barrier, inc=1, device_id={"col": other_c}, device_id_type=MESH)
+
+    def pack(ref, buf):
+        x = ref[...].astype(f32)
+        x = jnp.concatenate([x[:half_rows], x[half_rows:]], axis=-1)
+        buf[r, c, h] = jnp.zeros(buf.shape[3:], bf16)
+        buf[r, c, h, :, 0:cols, :] = x.astype(bf16)
+
+    pack(pair_ref, pbuf)
+    for p in range(2):
+        wbuf[h, p, 0:width, :] = jnp.concatenate([w_in_ref[2 * p], w_in_ref[2 * p + 1]], axis=-1)
+    wg = w_gate_ref[...]
+    wbuf[h, 0, width : width + width // 2, :] = jnp.concatenate(
+        [wg[: width // 2], wg[width // 2 :]], axis=-1
+    )
+    wbuf[h, 1, width : width + width // 2, :] = w_out_ref[...]
+    pack(cot_ref, cbuf)
+    pl.semaphore_wait(barrier, len(far) + 1)
+
+    def far_copy(buf, slot, send, recv, device):
+        return pltpu.make_async_remote_copy(
+            src_ref=buf.at[slot], dst_ref=buf.at[slot], send_sem=send, recv_sem=recv,
+            device_id=device, device_id_type=MESH,
+        )
+
+    def spread(buf, send, fwd, recv):
+        sent = []
+        own = (r, c, h)
+        for dr, dh in far:
+            pr, ph = place(dr, dh)
+            sent.append(
+                far_copy(buf, own, send.at[dr, dh], recv.at[own], {"row": pr, "chan": ph})
+            )
+        sent.append(far_copy(buf, own, fwd.at[0, 0], recv.at[own], {"col": other_c}))
+        for copy in sent:
+            copy.start()
+        return sent
+
+    def relay(buf, fwd, recv):
+        sent = []
+        for dr, dh in far:
+            pr, ph = place(dr, dh)
+            slot = (pr, c, ph)
+            copy = far_copy(buf, slot, fwd.at[dr, dh], recv.at[slot], {"col": other_c})
+            copy.wait_recv()
+            copy.start()
+            sent.append(copy)
+        return sent
+
+    def arrived(buf, fwd, recv):
+        for dr, dh in steps:
+            pr, ph = place(dr, dh)
+            slot = (pr, other_c, ph)
+            far_copy(buf, slot, fwd.at[dr, dh], recv.at[slot], {"col": other_c}).wait_recv()
+
+    sent = spread(pbuf, p_send, p_fwd, p_recv)
+    w_far = far_copy(wbuf, (h, c), w_send.at[0], w_recv.at[0], {"chan": other_h})
+    w_far.start()
+    sent += spread(cbuf, c_send, c_fwd, c_recv)
+
+    token = lax.broadcasted_iota(jnp.int32, (n, width), 0)
+    mj = jnp.zeros((n, width), f32)
+    for j in range(n):
+        mj = jnp.where(token == j, mask_ref[j].astype(f32), mj)
+    mj_s[...] = jnp.zeros(mj_s.shape, f32)
+    mj_s[0:n, :] = mj
+    tail = z_s.shape[0] - n * n
+    for s in (z_s, zh_s, l_s, r_s):
+        s[n * n : n * n + tail, :] = jnp.zeros((tail, width), f32)
+
+    sent += relay(pbuf, p_fwd, p_recv)
+    w_near = far_copy(wbuf, (other_h, c), w_send.at[1], w_recv.at[1], {"col": other_c})
+    far_copy(wbuf, (other_h, c), w_send.at[0], w_recv.at[0], {"chan": other_h}).wait_recv()
+    w_near.start()
+    sent += [w_far, w_near]
+    arrived(pbuf, p_fwd, p_recv)
+    far_copy(wbuf, (other_h, other_c), w_send.at[1], w_recv.at[1], {"col": other_c}).wait_recv()
+
+    w_in = []
+    for p in range(2):
+        w_in += [w.astype(bf16) for w in merge(wbuf[0, p, 0:width, :], wbuf[1, p, 0:width, :])]
+    last = slice(width, width + width // 2)
+    w_gate = jnp.concatenate(merge(wbuf[0, 0, last, :], wbuf[1, 0, last, :]), axis=0).astype(bf16)
+    w_out = jnp.concatenate([wbuf[0, 1, last, :], wbuf[1, 1, last, :]], axis=0)
+
+    def unpack(buf, dst, br):
+        for bc in range(2):
+            for part, full in enumerate(merge(buf[br, bc, 0], buf[br, bc, 1])):
+                for t in range(half_rows):
+                    start = (br * rows + part * half_rows + t) * n + bc * cols
+                    dst[start : start + cols, :] = full[t, 0:cols, :]
+
+    for br in range(n_row):
+        unpack(pbuf, z_s, br)
+        at = slice(br * block, (br + 1) * block)
+        z = z_s[at, :]
+        mean, rstd = norm_stats(z)
+        zh = (z - mean) * rstd
+        zh_s[at, :] = zh
+        zn = zh.astype(bf16)
+        pm = jnp.concatenate([mj * mask_ref[br * rows + t].astype(f32) for t in range(rows)], axis=0)
+        left = pm * sigmoid(dot(zn, w_in[1])) * dot(zn, w_in[0])
+        l_s[at, :] = left.astype(bf16).astype(f32)
+        right = pm * sigmoid(dot(zn, w_in[3])) * dot(zn, w_in[2])
+        r_s[at, :] = right.astype(bf16).astype(f32)
+
+    sent += relay(cbuf, c_fwd, c_recv)
+
+    def products(rows_ref, turned_ref):
+        def step(k, sums):
+            turned = turned_ref[pl.ds(k, n, stride=n), :]
+            return tuple(
+                s + rows_ref[pl.ds((r * rows + i) * n + k, 1), :] * turned
+                for i, s in enumerate(sums)
+            )
+
+        sums = lax.fori_loop(0, n, step, (jnp.zeros((n, width), f32),) * rows, unroll=4)
+        return jnp.concatenate(sums, axis=0)
+
+    tri_a = products(l_s, r_s)
+    tri_b = products(r_s, l_s)
+
+    arrived(cbuf, c_fwd, c_recv)
+    for br in range(n_row):
+        unpack(cbuf, c_s, br)
+
+    def turned_block(ref):
+        return jnp.concatenate(
+            [ref[pl.ds(r * rows + j, n, stride=n), :] for j in range(rows)], axis=0
+        )
+
+    def hidden(tri, zn, cot):
+        mean, rstd = norm_stats(tri)
+        xhat = (tri - mean) * rstd
+        proj_out = dot(xhat.astype(bf16), w_out)
+        gate = sigmoid(dot(zn, w_gate))
+        dxn = dot((cot * gate).astype(bf16), w_out, True)
+        dtri = (dxn - lane_mean(dxn) - xhat * lane_mean(dxn * xhat)) * rstd
+        return proj_out, gate, dtri.astype(bf16).astype(f32)
+
+    own_rows = pl.ds(pl.multiple_of(r * block, 8), block)
+    cot_a = c_s[own_rows, :]
+    proj_out, gate, dtri = hidden(tri_a, zh_s[own_rows, :].astype(bf16), cot_a)
+    da_s[...] = dtri
+    u_s[...] = jnp.zeros(u_s.shape, f32)
+    dg_s[...] = jnp.zeros(dg_s.shape, f32)
+    u_s[0:block, :] = gate * proj_out
+    dg_s[0:block, :] = cot_a * proj_out * gate * (1.0 - gate)
+    _, _, dtri = hidden(tri_b, turned_block(zh_s).astype(bf16), turned_block(c_s))
+    db_s[...] = dtri
+
+    def own_cells(ref, first):
+        return jnp.concatenate(
+            [ref[pl.ds((first + i) * n + c * cols, pad), :] for i in range(rows)], axis=0
+        )
+
+    def gradients(d_ref, other_ref):
+        def step(j, sums):
+            other = other_ref[pl.ds(j * n + c * cols, pad), :]
+            return tuple(s + d_ref[pl.ds(i * n + j, 1), :] * other for i, s in enumerate(sums))
+
+        sums = lax.fori_loop(0, n, step, (jnp.zeros((pad, width), f32),) * rows, unroll=4)
+        return jnp.concatenate(sums, axis=0)
+
+    dleft = gradients(da_s, r_s)
+    dright = gradients(db_s, l_s)
+
+    z = own_cells(z_s, r * rows)
+    mean, rstd = norm_stats(z)
+    zhat = (z - mean) * rstd
+    zn = zhat.astype(bf16)
+    own_mask = mj_s[pl.ds(c * cols, pad), :]
+    pm = jnp.concatenate(
+        [own_mask * mask_ref[r * rows + i].astype(f32) for i in range(rows)], axis=0
+    )
+    s1, s3 = sigmoid(dot(zn, w_in[1])), sigmoid(dot(zn, w_in[3]))
+    dpre = [
+        dleft * pm * s1,
+        dleft * pm * dot(zn, w_in[0]) * s1 * (1.0 - s1),
+        dright * pm * s3,
+        dright * pm * dot(zn, w_in[2]) * s3 * (1.0 - s3),
+    ]
+    dzn = dot(own_cells(dg_s, 0).astype(bf16), w_gate, True)
+    for q in range(4):
+        dzn = dzn + dot(dpre[q].astype(bf16), w_in[q], True)
+    grad = (dzn - lane_mean(dzn) - zhat * lane_mean(dzn * zhat)) * rstd
+
+    def put(ref, value):
+        value = jnp.where(h == 0, value, pltpu.roll(value, width // 2, 1))
+        value = value.reshape(rows, pad, width)[:, 0:cols, 0 : width // 2]
+        ref[...] = value.astype(bf16)
+
+    put(update_ref, own_cells(u_s, 0))
+    put(grad_ref, grad)
+    for copy in sent:
+        copy.wait_send()
+
+
+def gathered(n_row, pair, token_mask, w_in, w_gate, w_out, cotangent):
+    f32, bf16 = jnp.float32, jnp.bfloat16
+    rows, cols, chans = pair.shape
+    n = rows * n_row
+    width = 2 * chans
+    pad = -(-cols // 16) * 16
+    vmem = pl.BlockSpec(memory_space=pltpu.VMEM)
+    shards = pltpu.VMEM((n_row, 2, 2, rows // 2, pad, width), bf16)
+    cells = pltpu.VMEM((n * n + 8, width), f32)
+    block = pltpu.VMEM((rows * n, width), f32)
+    block_and_tail = pltpu.VMEM((rows * n + 8, width), f32)
+    dma = pltpu.SemaphoreType.DMA
+    out = jax.ShapeDtypeStruct(pair.shape, bf16)
+    return pl.pallas_call(
+        functools.partial(kernel, n_row),
+        out_shape=(out, out),
+        in_specs=[vmem, pl.BlockSpec(memory_space=pltpu.SMEM), vmem, vmem, vmem, vmem],
+        out_specs=(vmem, vmem),
+        scratch_shapes=[
+            shards, shards, pltpu.VMEM((2, 2, width + width // 2, width), bf16),
+            cells, cells, cells, cells, cells, pltpu.VMEM((n + 8, width), f32),
+            block_and_tail, block_and_tail, block, block,
+            dma((n_row, 2)), dma((n_row, 2)), dma((n_row, 2, 2)),
+            dma((n_row, 2)), dma((n_row, 2)), dma((n_row, 2, 2)),
+            dma((2,)), dma((2,)),
+        ],
+        compiler_params=pltpu.CompilerParams(
+            collective_id=0, has_side_effects=True, vmem_limit_bytes=24 * 2**20
+        ),
+    )(pair, token_mask, w_in.transpose(1, 0, 2), w_gate, w_out, cotangent)
 
 
 def body(pair, token_mask, w_in, w_gate, w_out, cotangent):
@@ -112,9 +402,20 @@
     return (update, pair_grad)
 
 
+def plan(pair, token_mask, w_in, w_gate, w_out, cotangent):
+    n_row, n_col, n_chan = (lax.axis_size(a) for a in ("row", "col", "chan"))
+    rows, cols, chans = pair.shape
+    n = token_mask.shape[0]
+    small = n <= 32 and n % 8 == 0 and rows % 2 == 0 and cols % 4 == 0 and rows * n % 16 == 0
+    shaped = n_col == 2 and n_chan == 2 and chans == 64 and w_in.shape == (128, 4, 64)
+    if small and shaped and -(-cols // 16) * 16 - cols <= 8:
+        return gathered(n_row, pair, token_mask, w_in, w_gate, w_out, cotangent)
+    return body(pair, token_mask, w_in, w_gate, w_out, cotangent)
+
+
 def solution(mesh):
     return jax.shard_map(
-        body,
+        plan,
         mesh=mesh,
         in_specs=(
             P(("groups", "row"), "col", "chan"),

time: 113 us -> 19.8 us (0.18)
  blocking collectives: 57.2 us -> 0 us
  waiting for transfers between devices: 22.1 us -> 0 us
  Pallas kernels: 0 us -> 15.2 us
  between operations: 14 us -> 0.7 us
  local copies, waits for them, and re-layouts: 9.73 us -> 3.66 us
  starting transfers between devices: 4.58 us -> 0 us
  matrix products: 2.66 us -> 0 us
  other arithmetic: 2.55 us -> 0 us
    all_gather x5 -> x0, blocking collectives: 42.1 us -> none  [the longest x1 13.8 us: body(): lax.all_gather(right, 'row', axis=0, tiled=True)]
    pallas_call x0 -> x1, Pallas kernels: none -> 15.2 us  [gathered(): pl.pallas_call(functools.partial(kernel, n_row), out_shape=(out, out), in...]
    psum x3 -> x0, blocking collectives: 15.1 us -> none  [the longest x1 5.11 us: body(): lax.psum((jnp.sum(triangle_product, axis=-1), jnp.sum(triangle_product *...]
    reduce_scatter x1 -> x0, waiting for transfers between devices: 8.56 us -> none  [body(): lax.psum_scatter(partial_tri, 'col', scatter_dimension=1, tiled=True)]
    unnamed x5 -> x0, waiting for transfers between devices: 8.25 us -> none
    all_to_all x1 -> x0, waiting for transfers between devices: 5.24 us -> none  [body(): lax.all_to_all(dtri_rows, 'row', split_axis=1, concat_axis=0, tiled=True)]
    all_to_all x1 -> x0, starting transfers between devices: 4.5 us -> none  [body(): lax.all_to_all(dtri_rows, 'row', split_axis=1, concat_axis=0, tiled=True)]
    unnamed x25 -> x12, local copies, waits for them, and re-layouts: 6.89 us -> 3.66 us
  transfers between devices with their start and end apart: 4 -> 0, of which waited for: 3 -> 0; matrix products, arithmetic and copies ran while one was open for 1% -> 0% of each run, Pallas kernels for 0% -> 0%
where the time goes in v1:
time: 19.8 us; the launch traced here: 19.6 us
  Pallas kernels  15.2 us (77%)
  local copies, waits for them, and re-layouts  3.66 us (18%)
  between operations  0.7 us (4%)
    pallas_call x1, Pallas kernels, gathered(): pl.pallas_call(functools.partial(kernel, n_row), out_shape=(out, out), in...  15.2 us
    unnamed x12, local copies, waits for them, and re-layouts  3.66 us

profile of v1, /device:TPU:0, one launch (start us, length us, event | category | flops | bytes accessed | tf_op | source)
XLA Modules:
  0.0 19.6 jit_solution(11967728011220789860)
XLA Ops:
  0.6 0.8 %copy.9.w_gate_ref = bf16[128,64]{1,0:T(8,128)(2,1)S(1)} copy(bf16[128,64]{0,1:T(8,128)(2,1)} %param.9) | data formatting | bytes 32768 | tf_op args[3]
  1.5 0.0 copy-start
  1.5 0.0 copy-start.1
  1.5 0.0 copy-start.2
  1.5 1.0 %copy.8 = bf16[128,4,64]{2,0,1:T(8,128)(2,1)S(1)} copy(bf16[128,4,64]{0,2,1:T(8,128)(2,1)} %param.8) | data formatting | bytes 131072 | tf_op args[2]
  2.5 0.0 copy-start.3
  2.5 0.0 copy-done
  2.5 0.0 copy-done.1
  2.5 0.0 copy-done.2
  2.5 0.6 %copy-done.3 = s32[24]{0:T(128)S(1)} copy-done((s32[24]{0:T(128)S(1)}, s32[24]{0:T(128)}, u32[]{:S(2)}) %copy-start.3) | copy-done | bytes 120
  3.1 15.2 %shard_map.77 = (bf16[6,12,64]{2,1,0:T(8,128)(2,1)S(1)}, bf16[6,12,64]{2,1,0:T(8,128)(2,1)S(1)}) custom-call(bf16[6,12,64]{2,1,0:T(8,128)(2,1)S(1)} %copy-done, s32[24]{0:T(128)S(1)} %copy-done.3, bf16[4,128,64]{2,1,0:T(8,128)(2,1)S(1)} %bitcast.1, bf16[128,64]{1,0:T(8,128)(2,1)S(1)} %copy.9.w_gate_ref, bf16[64,128]{1,0:T(8,128)(2,1)S(1)} %copy-done.2, ...), custom_call_target="tpu_custom_call" | custom-call | tf_op jit(solution)/shard_map/pallas_call | solution.py:280
  18.4 0.6 %copy.12 = bf16[6,12,64]{2,1,0:T(8,128)(2,1)} copy(bf16[6,12,64]{2,1,0:T(8,128)(2,1)S(1)} %get-tuple-element.4) | data formatting | bytes 18432
  19.0 0.6 %copy.13 = bf16[6,12,64]{2,1,0:T(8,128)(2,1)} copy(bf16[6,12,64]{2,1,0:T(8,128)(2,1)S(1)} %get-tuple-element.5) | data formatting | bytes 18432
Async XLA Ops:
  1.5 1.0 %copy-start = (bf16[6,12,64]{2,1,0:T(8,128)(2,1)S(1)}, bf16[6,12,64]{2,1,0:T(8,128)(2,1)}, u32[]{:S(2)}) copy-start(bf16[6,12,64]{2,1,0:T(8,128)(2,1)} %pair_ref.1) | copy-start | bytes 27652
  1.5 1.0 %copy-start.1 = (bf16[6,12,64]{2,1,0:T(8,128)(2,1)S(1)}, bf16[6,12,64]{2,1,0:T(8,128)(2,1)}, u32[]{:S(2)}) copy-start(bf16[6,12,64]{2,1,0:T(8,128)(2,1)} %cot_ref.1) | copy-start | bytes 27652
  1.5 1.0 %copy-start.2 = (bf16[64,128]{1,0:T(8,128)(2,1)S(1)}, bf16[64,128]{1,0:T(8,128)(2,1)}, u32[]{:S(2)}) copy-start(bf16[64,128]{1,0:T(8,128)(2,1)} %w_out_ref.1) | copy-start | bytes 49156
  2.5 0.7 %copy-start.3 = (s32[24]{0:T(128)S(1)}, s32[24]{0:T(128)}, u32[]{:S(2)}) copy-start(s32[24]{0:T(128)} %mask_ref.1) | copy-start | bytes 292

commit v2 on v1

--- a/solution.py
+++ b/solution.py
@@ -42,8 +42,8 @@
 
 
 def kernel(
-    n_row, pair_ref, mask_ref, w_in_ref, w_gate_ref, w_out_ref, cot_ref, update_ref, grad_ref,
-    pbuf, cbuf, wbuf, z_s, zh_s, c_s, l_s, r_s, mj_s, u_s, dg_s, da_s, db_s,
+    n_row, pair_hbm, mask_hbm, w_in_hbm, w_gate_hbm, w_out_hbm, cot_hbm, out_ref,
+    pair_ref, cot_ref, mask_ref, in_sem, pbuf, cbuf, wbuf, z_s, zh_s, c_s, l_s, r_s, mj_s, u_s, dg_s, da_s, db_s,
     p_send, p_fwd, p_recv, c_send, c_fwd, c_recv, w_send, w_recv,
 ):
     f32, bf16 = jnp.float32, jnp.bfloat16
@@ -62,6 +62,24 @@
     steps = [(dr, dh) for dr in range(n_row) for dh in range(2)]
     far = [s for s in steps if s != (0, 0)]
 
+    mine = pl.ds(pl.multiple_of(h * (width // 2), width // 2), width // 2)
+    loads = [
+        pltpu.make_async_copy(src, dst, in_sem.at[i])
+        for i, (src, dst) in enumerate(
+            [
+                (pair_hbm, pair_ref),
+                (w_in_hbm.at[0:2], wbuf.at[0:2, mine]),
+                (w_gate_hbm, wbuf.at[2, mine]),
+                (w_in_hbm.at[2:4], wbuf.at[3:5, mine]),
+                (w_out_hbm, wbuf.at[5, mine]),
+                (cot_hbm, cot_ref),
+                (mask_hbm, mask_ref),
+            ]
+        )
+    ]
+    for load in loads:
+        load.start()
+
     barrier = pltpu.get_barrier_semaphore()
     for dr, dh in far:
         pr, ph = place(dr, dh)
@@ -74,15 +92,8 @@
         buf[r, c, h] = jnp.zeros(buf.shape[3:], bf16)
         buf[r, c, h, :, 0:cols, :] = x.astype(bf16)
 
+    loads[0].wait()
     pack(pair_ref, pbuf)
-    for p in range(2):
-        wbuf[h, p, 0:width, :] = jnp.concatenate([w_in_ref[2 * p], w_in_ref[2 * p + 1]], axis=-1)
-    wg = w_gate_ref[...]
-    wbuf[h, 0, width : width + width // 2, :] = jnp.concatenate(
-        [wg[: width // 2], wg[width // 2 :]], axis=-1
-    )
-    wbuf[h, 1, width : width + width // 2, :] = w_out_ref[...]
-    pack(cot_ref, cbuf)
     pl.semaphore_wait(barrier, len(far) + 1)
 
     def far_copy(buf, slot, send, recv, device):
@@ -122,10 +133,20 @@
             far_copy(buf, slot, fwd.at[dr, dh], recv.at[slot], {"col": other_c}).wait_recv()
 
     sent = spread(pbuf, p_send, p_fwd, p_recv)
-    w_far = far_copy(wbuf, (h, c), w_send.at[0], w_recv.at[0], {"chan": other_h})
+    for load in loads[1:5]:
+        load.wait()
+
+    def weights(core, rows):
+        return (pl.ds(3 * core, 3), rows)
+
+    theirs = pl.ds(pl.multiple_of(other_h * (width // 2), width // 2), width // 2)
+    w_far = far_copy(wbuf, weights(c, mine), w_send.at[0], w_recv.at[0], {"chan": other_h})
     w_far.start()
+    loads[5].wait()
+    pack(cot_ref, cbuf)
     sent += spread(cbuf, c_send, c_fwd, c_recv)
 
+    loads[6].wait()
     token = lax.broadcasted_iota(jnp.int32, (n, width), 0)
     mj = jnp.zeros((n, width), f32)
     for j in range(n):
@@ -137,19 +158,16 @@
         s[n * n : n * n + tail, :] = jnp.zeros((tail, width), f32)
 
     sent += relay(pbuf, p_fwd, p_recv)
-    w_near = far_copy(wbuf, (other_h, c), w_send.at[1], w_recv.at[1], {"col": other_c})
-    far_copy(wbuf, (other_h, c), w_send.at[0], w_recv.at[0], {"chan": other_h}).wait_recv()
+    w_near = far_copy(wbuf, weights(c, theirs), w_send.at[1], w_recv.at[1], {"col": other_c})
+    far_copy(wbuf, weights(c, theirs), w_send.at[0], w_recv.at[0], {"chan": other_h}).wait_recv()
     w_near.start()
     sent += [w_far, w_near]
     arrived(pbuf, p_fwd, p_recv)
-    far_copy(wbuf, (other_h, other_c), w_send.at[1], w_recv.at[1], {"col": other_c}).wait_recv()
-
-    w_in = []
-    for p in range(2):
-        w_in += [w.astype(bf16) for w in merge(wbuf[0, p, 0:width, :], wbuf[1, p, 0:width, :])]
-    last = slice(width, width + width // 2)
-    w_gate = jnp.concatenate(merge(wbuf[0, 0, last, :], wbuf[1, 0, last, :]), axis=0).astype(bf16)
-    w_out = jnp.concatenate([wbuf[0, 1, last, :], wbuf[1, 1, last, :]], axis=0)
+    far_copy(wbuf, weights(other_c, theirs), w_send.at[1], w_recv.at[1], {"col": other_c}).wait_recv()
+
+    w_left = wbuf[0:2].reshape(2 * width, width)
+    w_right = wbuf[3:5].reshape(2 * width, width)
+    w_gate, w_out = wbuf[2], wbuf[5]
 
     def unpack(buf, dst, br):
         for bc in range(2):
@@ -167,9 +185,11 @@
         zh_s[at, :] = zh
         zn = zh.astype(bf16)
         pm = jnp.concatenate([mj * mask_ref[br * rows + t].astype(f32) for t in range(rows)], axis=0)
-        left = pm * sigmoid(dot(zn, w_in[1])) * dot(zn, w_in[0])
+        proj = dot(zn, w_left, True)
+        left = pm * sigmoid(proj[:, width:]) * proj[:, :width]
         l_s[at, :] = left.astype(bf16).astype(f32)
-        right = pm * sigmoid(dot(zn, w_in[3])) * dot(zn, w_in[2])
+        proj = dot(zn, w_right, True)
+        right = pm * sigmoid(proj[:, width:]) * proj[:, :width]
         r_s[at, :] = right.astype(bf16).astype(f32)
 
     sent += relay(cbuf, c_fwd, c_recv)
@@ -201,7 +221,7 @@
         mean, rstd = norm_stats(tri)
         xhat = (tri - mean) * rstd
         proj_out = dot(xhat.astype(bf16), w_out)
-        gate = sigmoid(dot(zn, w_gate))
+        gate = sigmoid(dot(zn, w_gate, True))
         dxn = dot((cot * gate).astype(bf16), w_out, True)
         dtri = (dxn - lane_mean(dxn) - xhat * lane_mean(dxn * xhat)) * rstd
         return proj_out, gate, dtri.astype(bf16).astype(f32)
@@ -241,25 +261,17 @@
     pm = jnp.concatenate(
         [own_mask * mask_ref[r * rows + i].astype(f32) for i in range(rows)], axis=0
     )
-    s1, s3 = sigmoid(dot(zn, w_in[1])), sigmoid(dot(zn, w_in[3]))
-    dpre = [
-        dleft * pm * s1,
-        dleft * pm * dot(zn, w_in[0]) * s1 * (1.0 - s1),
-        dright * pm * s3,
-        dright * pm * dot(zn, w_in[2]) * s3 * (1.0 - s3),
-    ]
-    dzn = dot(own_cells(dg_s, 0).astype(bf16), w_gate, True)
-    for q in range(4):
-        dzn = dzn + dot(dpre[q].astype(bf16), w_in[q], True)
+    dzn = dot(own_cells(dg_s, 0).astype(bf16), w_gate)
+    for grads, w in ((dleft, w_left), (dright, w_right)):
+        proj = dot(zn, w, True)
+        gated = sigmoid(proj[:, width:])
+        dpre = [grads * pm * gated, grads * pm * proj[:, :width] * gated * (1.0 - gated)]
+        dzn = dzn + dot(jnp.concatenate(dpre, axis=1).astype(bf16), w)
     grad = (dzn - lane_mean(dzn) - zhat * lane_mean(dzn * zhat)) * rstd
 
-    def put(ref, value):
+    for i, value in enumerate((own_cells(u_s, 0), grad)):
         value = jnp.where(h == 0, value, pltpu.roll(value, width // 2, 1))
-        value = value.reshape(rows, pad, width)[:, 0:cols, 0 : width // 2]
-        ref[...] = value.astype(bf16)
-
-    put(update_ref, own_cells(u_s, 0))
-    put(grad_ref, grad)
+        out_ref[i] = value.reshape(rows, pad, width)[:, 0:cols, 0 : width // 2].astype(bf16)
     for copy in sent:
         copy.wait_send()
 
@@ -276,14 +288,15 @@
     block = pltpu.VMEM((rows * n, width), f32)
     block_and_tail = pltpu.VMEM((rows * n + 8, width), f32)
     dma = pltpu.SemaphoreType.DMA
-    out = jax.ShapeDtypeStruct(pair.shape, bf16)
-    return pl.pallas_call(
+    out = pl.pallas_call(
         functools.partial(kernel, n_row),
-        out_shape=(out, out),
-        in_specs=[vmem, pl.BlockSpec(memory_space=pltpu.SMEM), vmem, vmem, vmem, vmem],
-        out_specs=(vmem, vmem),
+        out_shape=jax.ShapeDtypeStruct((2,) + pair.shape, bf16),
+        in_specs=[pl.BlockSpec(memory_space=pltpu.HBM)] * 6,
+        out_specs=vmem,
         scratch_shapes=[
-            shards, shards, pltpu.VMEM((2, 2, width + width // 2, width), bf16),
+            pltpu.VMEM(pair.shape, bf16), pltpu.VMEM(pair.shape, bf16),
+            pltpu.SMEM(token_mask.shape, jnp.int32), dma((7,)),
+            shards, shards, pltpu.VMEM((6, width, width), bf16),
             cells, cells, cells, cells, cells, pltpu.VMEM((n + 8, width), f32),
             block_and_tail, block_and_tail, block, block,
             dma((n_row, 2)), dma((n_row, 2)), dma((n_row, 2, 2)),
@@ -291,9 +304,10 @@
             dma((2,)), dma((2,)),
         ],
         compiler_params=pltpu.CompilerParams(
-            collective_id=0, has_side_effects=True, vmem_limit_bytes=24 * 2**20
+            collective_id=0, has_side_effects=True, vmem_limit_bytes=60 * 2**20
         ),
-    )(pair, token_mask, w_in.transpose(1, 0, 2), w_gate, w_out, cotangent)
+    )(pair, token_mask, w_in.transpose(1, 2, 0), w_gate.T, w_out, cotangent)
+    return out[0], out[1]
 
 
 def body(pair, token_mask, w_in, w_gate, w_out, cotangent):

time: 19.8 us -> 17.7 us (0.89)
  local copies, waits for them, and re-layouts: 3.66 us -> 1.38 us
  Pallas kernels: 15.2 us -> 15.5 us
    unnamed x12 -> x0, local copies, waits for them, and re-layouts: 3.66 us -> none
    squeeze x0 -> x1, local copies, waits for them, and re-layouts: none -> 1.38 us  [gathered(): return (out[0], out[1])]
    pallas_call x1, Pallas kernels: 15.2 us -> 15.5 us  [gathered(): pl.pallas_call(functools.partial(kernel, n_row), out_shape=jax.ShapeDtype...]
where the time goes in v2:
time: 17.7 us; the launch traced here: 17.5 us
  Pallas kernels  15.5 us (88%)
  local copies, waits for them, and re-layouts  1.38 us (8%)
  between operations  0.64 us (4%)
    pallas_call x1, Pallas kernels, gathered(): pl.pallas_call(functools.partial(kernel, n_row), out_shape=jax.ShapeDtype...  15.5 us
    squeeze x1, local copies, waits for them, and re-layouts, gathered(): return (out[0], out[1])  1.38 us

profile of v2, /device:TPU:0, one launch (start us, length us, event | category | flops | bytes accessed | tf_op | source)
XLA Modules:
  0.0 17.5 jit_solution(9006658858499112015)
XLA Ops:
  0.6 15.5 %shard_map.77 = bf16[2,6,12,64]{3,2,1,0:T(8,128)(2,1)} custom-call(bf16[6,12,64]{2,1,0:T(8,128)(2,1)} %pair_hbm.1, s32[24]{0:T(128)} %mask_hbm.1, bf16[4,64,128]{2,1,0:T(8,128)(2,1)} %bitcast.6, bf16[64,128]{1,0:T(8,128)(2,1)} %bitcast.7, bf16[64,128]{1,0:T(8,128)(2,1)} %w_out_hbm.1, bf16[6,12,64]{2,1,0:T(8,128)(2,1)} %cot_hbm.1), custom_call_target="tpu_custom_call" | custom-call | tf_op jit(solution)/shard_map/pallas_call | solution.py:291
  16.1 1.4 %slice_bitcast_fusion = (bf16[6,12,64]{2,1,0:T(8,128)(2,1)}, bf16[6,12,64]{2,1,0:T(8,128)(2,1)}) fusion(bf16[2,6,12,64]{3,2,1,0:T(8,128)(2,1)} %shard_map.77), kind=kLoop, calls=%fused_computation | loop fusion | bytes 36864 | tf_op jit(solution)/shard_map/squeeze | solution.py:310

commit v3 on v2

--- a/solution.py
+++ b/solution.py
@@ -55,6 +55,12 @@
     block = rows * n
     r, c, h = lax.axis_index("row"), lax.axis_index("col"), lax.axis_index("chan")
     other_c, other_h = 1 - c, 1 - h
+    wanted_c = lax.div(r * rows, cols)
+    plane = [(0, 1), (1, 0), (1, 1)]
+
+    def partner(dc, dh):
+        return lax.rem(c + dc, 2), lax.rem(h + dh, 2)
+
 
     def place(dr, dh):
         return lax.rem(r + dr, n_row), lax.rem(h + dh, 2)
@@ -81,10 +87,11 @@
         load.start()
 
     barrier = pltpu.get_barrier_semaphore()
-    for dr, dh in far:
-        pr, ph = place(dr, dh)
-        pl.semaphore_signal(barrier, inc=1, device_id={"row": pr, "chan": ph}, device_id_type=MESH)
-    pl.semaphore_signal(barrier, inc=1, device_id={"col": other_c}, device_id_type=MESH)
+    everyone = [(dr, 0, dh) for dr, dh in far] + [(0, 1, 0)]
+    for dr, dc, dh in everyone:
+        pc, ph = partner(dc, dh)
+        device = {"row": lax.rem(r + dr, n_row), "col": pc, "chan": ph}
+        pl.semaphore_signal(barrier, inc=1, device_id=device, device_id_type=MESH)
 
     def pack(ref, buf):
         x = ref[...].astype(f32)
@@ -94,7 +101,7 @@
 
     loads[0].wait()
     pack(pair_ref, pbuf)
-    pl.semaphore_wait(barrier, len(far) + 1)
+    pl.semaphore_wait(barrier, len(everyone))
 
     def far_copy(buf, slot, send, recv, device):
         return pltpu.make_async_remote_copy(
@@ -115,22 +122,48 @@
             copy.start()
         return sent
 
-    def relay(buf, fwd, recv):
-        sent = []
-        for dr, dh in far:
+    def relay(buf, fwd, recv, dr):
+        for dh in range(2):
+            if (dr, dh) == (0, 0):
+                continue
             pr, ph = place(dr, dh)
             slot = (pr, c, ph)
             copy = far_copy(buf, slot, fwd.at[dr, dh], recv.at[slot], {"col": other_c})
             copy.wait_recv()
             copy.start()
             sent.append(copy)
-        return sent
-
-    def arrived(buf, fwd, recv):
-        for dr, dh in steps:
-            pr, ph = place(dr, dh)
-            slot = (pr, other_c, ph)
-            far_copy(buf, slot, fwd.at[dr, dh], recv.at[slot], {"col": other_c}).wait_recv()
+
+    def wait_for(buf, recv, slot):
+        far_copy(buf, slot, w_send.at[0], recv.at[slot], {"col": other_c}).wait_recv()
+
+    def cot_copies(act):
+        own = (r, c, h)
+        for dr in range(n_row):
+            pr = lax.rem(r + dr, n_row)
+
+            def to_plane():
+                for dc, dh in [(0, 0), (0, 1)] if dr else [(0, 1), (1, 0)]:
+                    pc, ph = partner(dc, dh)
+                    device = {"row": pr, "col": pc, "chan": ph}
+                    act(far_copy(cbuf, own, c_send.at[dr, dc, dh], c_recv.at[own], device))
+
+            if dr:
+                pl.when(lax.div(pr * rows, cols) == c)(to_plane)
+            else:
+                to_plane()
+
+    def cot_relay(act):
+        def pass_on(dr, dh):
+            slot = (lax.rem(r + dr, n_row), c, lax.rem(h + dh, 2))
+            act(far_copy(cbuf, slot, c_fwd.at[dr, dh], c_recv.at[slot], {"col": other_c}))
+
+        pass_on(0, 1)
+
+        @pl.when(c == wanted_c)
+        def _():
+            for dr in range(1, n_row):
+                for dh in range(2):
+                    pass_on(dr, dh)
 
     sent = spread(pbuf, p_send, p_fwd, p_recv)
     for load in loads[1:5]:
@@ -144,7 +177,7 @@
     w_far.start()
     loads[5].wait()
     pack(cot_ref, cbuf)
-    sent += spread(cbuf, c_send, c_fwd, c_recv)
+    cot_copies(lambda copy: copy.start())
 
     loads[6].wait()
     token = lax.broadcasted_iota(jnp.int32, (n, width), 0)
@@ -157,28 +190,32 @@
     for s in (z_s, zh_s, l_s, r_s):
         s[n * n : n * n + tail, :] = jnp.zeros((tail, width), f32)
 
-    sent += relay(pbuf, p_fwd, p_recv)
+    relay(pbuf, p_fwd, p_recv, 0)
     w_near = far_copy(wbuf, weights(c, theirs), w_send.at[1], w_recv.at[1], {"col": other_c})
     far_copy(wbuf, weights(c, theirs), w_send.at[0], w_recv.at[0], {"chan": other_h}).wait_recv()
     w_near.start()
     sent += [w_far, w_near]
-    arrived(pbuf, p_fwd, p_recv)
+    for dr in range(1, n_row):
+        relay(pbuf, p_fwd, p_recv, dr)
     far_copy(wbuf, weights(other_c, theirs), w_send.at[1], w_recv.at[1], {"col": other_c}).wait_recv()
 
     w_left = wbuf[0:2].reshape(2 * width, width)
     w_right = wbuf[3:5].reshape(2 * width, width)
     w_gate, w_out = wbuf[2], wbuf[5]
 
-    def unpack(buf, dst, br):
+    def unpack(buf, dst, br, bc):
+        for part, full in enumerate(merge(buf[br, bc, 0], buf[br, bc, 1])):
+            for t in range(half_rows):
+                first = pl.multiple_of(br * block, 8) + (part * half_rows + t) * n + bc * cols
+                dst[pl.ds(first, cols), :] = full[t, 0:cols, :]
+
+    for dr in range(n_row):
+        br = lax.rem(r + dr, n_row)
+        for dh in range(2):
+            wait_for(pbuf, p_recv, (br, other_c, lax.rem(h + dh, 2)))
         for bc in range(2):
-            for part, full in enumerate(merge(buf[br, bc, 0], buf[br, bc, 1])):
-                for t in range(half_rows):
-                    start = (br * rows + part * half_rows + t) * n + bc * cols
-                    dst[start : start + cols, :] = full[t, 0:cols, :]
-
-    for br in range(n_row):
-        unpack(pbuf, z_s, br)
-        at = slice(br * block, (br + 1) * block)
+            unpack(pbuf, z_s, br, bc)
+        at = pl.ds(pl.multiple_of(br * block, 8), block)
         z = z_s[at, :]
         mean, rstd = norm_stats(z)
         zh = (z - mean) * rstd
@@ -192,66 +229,56 @@
         right = pm * sigmoid(proj[:, width:]) * proj[:, :width]
         r_s[at, :] = right.astype(bf16).astype(f32)
 
-    sent += relay(cbuf, c_fwd, c_recv)
-
-    def products(rows_ref, turned_ref):
-        def step(k, sums):
+    def received_and_passed(copy):
+        copy.wait_recv()
+        copy.start()
+
+    cot_relay(received_and_passed)
+
+    def products(step, start):
+        sums = lax.fori_loop(0, n, step, ((start,) * rows,) * 2, unroll=24)
+        return [jnp.concatenate(s, axis=0) for s in sums]
+
+    def tri_step(k, sums):
+        out = []
+        for rows_ref, turned_ref, parts in ((l_s, r_s, sums[0]), (r_s, l_s, sums[1])):
             turned = turned_ref[pl.ds(k, n, stride=n), :]
-            return tuple(
+            out.append(tuple(
                 s + rows_ref[pl.ds((r * rows + i) * n + k, 1), :] * turned
-                for i, s in enumerate(sums)
-            )
-
-        sums = lax.fori_loop(0, n, step, (jnp.zeros((n, width), f32),) * rows, unroll=4)
-        return jnp.concatenate(sums, axis=0)
-
-    tri_a = products(l_s, r_s)
-    tri_b = products(r_s, l_s)
-
-    arrived(cbuf, c_fwd, c_recv)
-    for br in range(n_row):
-        unpack(cbuf, c_s, br)
+                for i, s in enumerate(parts)
+            ))
+        return tuple(out)
+
+    tri_a, tri_b = products(tri_step, jnp.zeros((n, width), f32))
 
     def turned_block(ref):
         return jnp.concatenate(
             [ref[pl.ds(r * rows + j, n, stride=n), :] for j in range(rows)], axis=0
         )
 
-    def hidden(tri, zn, cot):
+    def own_cells(ref, first):
+        return jnp.concatenate(
+            [ref[pl.ds((first + i) * n + c * cols, pad), :] for i in range(rows)], axis=0
+        )
+
+    def forward(tri, zn):
         mean, rstd = norm_stats(tri)
         xhat = (tri - mean) * rstd
         proj_out = dot(xhat.astype(bf16), w_out)
         gate = sigmoid(dot(zn, w_gate, True))
+        return xhat, rstd, proj_out, gate
+
+    def backward(xhat, rstd, gate, cot):
         dxn = dot((cot * gate).astype(bf16), w_out, True)
         dtri = (dxn - lane_mean(dxn) - xhat * lane_mean(dxn * xhat)) * rstd
-        return proj_out, gate, dtri.astype(bf16).astype(f32)
+        return dtri.astype(bf16).astype(f32)
 
     own_rows = pl.ds(pl.multiple_of(r * block, 8), block)
-    cot_a = c_s[own_rows, :]
-    proj_out, gate, dtri = hidden(tri_a, zh_s[own_rows, :].astype(bf16), cot_a)
-    da_s[...] = dtri
-    u_s[...] = jnp.zeros(u_s.shape, f32)
-    dg_s[...] = jnp.zeros(dg_s.shape, f32)
-    u_s[0:block, :] = gate * proj_out
-    dg_s[0:block, :] = cot_a * proj_out * gate * (1.0 - gate)
-    _, _, dtri = hidden(tri_b, turned_block(zh_s).astype(bf16), turned_block(c_s))
-    db_s[...] = dtri
-
-    def own_cells(ref, first):
-        return jnp.concatenate(
-            [ref[pl.ds((first + i) * n + c * cols, pad), :] for i in range(rows)], axis=0
-        )
-
-    def gradients(d_ref, other_ref):
-        def step(j, sums):
-            other = other_ref[pl.ds(j * n + c * cols, pad), :]
-            return tuple(s + d_ref[pl.ds(i * n + j, 1), :] * other for i, s in enumerate(sums))
-
-        sums = lax.fori_loop(0, n, step, (jnp.zeros((pad, width), f32),) * rows, unroll=4)
-        return jnp.concatenate(sums, axis=0)
-
-    dleft = gradients(da_s, r_s)
-    dright = gradients(db_s, l_s)
+    xhat_a, rstd_a, proj_out, gate_a = forward(tri_a, zh_s[own_rows, :].astype(bf16))
+    xhat_b, rstd_b, _, gate_b = forward(tri_b, turned_block(zh_s).astype(bf16))
+    u_s[0:block, :] = gate_a * proj_out
+    u_s[block:, :] = jnp.zeros((u_s.shape[0] - block, width), f32)
+    dg_s[block:, :] = jnp.zeros((u_s.shape[0] - block, width), f32)
 
     z = own_cells(z_s, r * rows)
     mean, rstd = norm_stats(z)
@@ -261,19 +288,52 @@
     pm = jnp.concatenate(
         [own_mask * mask_ref[r * rows + i].astype(f32) for i in range(rows)], axis=0
     )
-    dzn = dot(own_cells(dg_s, 0).astype(bf16), w_gate)
-    for grads, w in ((dleft, w_left), (dright, w_right)):
+    factors = []
+    for w in (w_left, w_right):
         proj = dot(zn, w, True)
-        gated = sigmoid(proj[:, width:])
-        dpre = [grads * pm * gated, grads * pm * proj[:, :width] * gated * (1.0 - gated)]
-        dzn = dzn + dot(jnp.concatenate(dpre, axis=1).astype(bf16), w)
-    grad = (dzn - lane_mean(dzn) - zhat * lane_mean(dzn * zhat)) * rstd
-
-    for i, value in enumerate((own_cells(u_s, 0), grad)):
+        gated = pm * sigmoid(proj[:, width:])
+        factors.append((gated, proj[:, :width] * gated * (1.0 - gated)))
+
+    def put(i, value):
         value = jnp.where(h == 0, value, pltpu.roll(value, width // 2, 1))
         out_ref[i] = value.reshape(rows, pad, width)[:, 0:cols, 0 : width // 2].astype(bf16)
+
+    put(0, own_cells(u_s, 0))
+
+    for bh in range(2):
+        wait_for(cbuf, c_recv, (r, other_c, bh))
+    for bc in range(2):
+        unpack(cbuf, c_s, r, bc)
+    for dr in range(1, n_row):
+        br = lax.rem(r + dr, n_row)
+        for bh in range(2):
+            slot = (br, wanted_c, bh)
+            pl.when(c != wanted_c)(functools.partial(wait_for, cbuf, c_recv, slot))
+        unpack(cbuf, c_s, br, wanted_c)
+
+    cot_a = c_s[own_rows, :]
+    dg_s[0:block, :] = cot_a * proj_out * gate_a * (1.0 - gate_a)
+    da_s[...] = backward(xhat_a, rstd_a, gate_a, cot_a)
+    db_s[...] = backward(xhat_b, rstd_b, gate_b, turned_block(c_s))
+
+    def gradient_step(j, sums):
+        out = []
+        for d_ref, other_ref, parts in ((da_s, r_s, sums[0]), (db_s, l_s, sums[1])):
+            other = other_ref[pl.ds(j * n + c * cols, pad), :]
+            out.append(tuple(
+                s + d_ref[pl.ds(i * n + j, 1), :] * other for i, s in enumerate(parts)
+            ))
+        return tuple(out)
+
+    grads = products(gradient_step, jnp.zeros((pad, width), f32))
+    dzn = dot(own_cells(dg_s, 0).astype(bf16), w_gate)
+    for grad, (value, gate), w in zip(grads, factors, (w_left, w_right)):
+        dzn = dzn + dot(jnp.concatenate([grad * value, grad * gate], axis=1).astype(bf16), w)
+    put(1, (dzn - lane_mean(dzn) - zhat * lane_mean(dzn * zhat)) * rstd)
     for copy in sent:
         copy.wait_send()
+    cot_copies(lambda copy: copy.wait_send())
+    cot_relay(lambda copy: copy.wait_send())
 
 
 def gathered(n_row, pair, token_mask, w_in, w_gate, w_out, cotangent):
@@ -288,9 +348,11 @@
     block = pltpu.VMEM((rows * n, width), f32)
     block_and_tail = pltpu.VMEM((rows * n + 8, width), f32)
     dma = pltpu.SemaphoreType.DMA
+    args = (pair, token_mask, w_in.transpose(1, 2, 0), w_gate.T, w_out, cotangent)
+    args = [pltpu.with_memory_space_constraint(a, pltpu.HBM) for a in args]
     out = pl.pallas_call(
         functools.partial(kernel, n_row),
-        out_shape=jax.ShapeDtypeStruct((2,) + pair.shape, bf16),
+        out_shape=pltpu.VMEM((2,) + pair.shape, bf16),
         in_specs=[pl.BlockSpec(memory_space=pltpu.HBM)] * 6,
         out_specs=vmem,
         scratch_shapes=[
@@ -300,13 +362,13 @@
             cells, cells, cells, cells, cells, pltpu.VMEM((n + 8, width), f32),
             block_and_tail, block_and_tail, block, block,
             dma((n_row, 2)), dma((n_row, 2)), dma((n_row, 2, 2)),
-            dma((n_row, 2)), dma((n_row, 2)), dma((n_row, 2, 2)),
+            dma((n_row, 2, 2)), dma((n_row, 2)), dma((n_row, 2, 2)),
             dma((2,)), dma((2,)),
         ],
         compiler_params=pltpu.CompilerParams(
-            collective_id=0, has_side_effects=True, vmem_limit_bytes=60 * 2**20
+            collective_id=0, has_side_effects=True, vmem_limit_bytes=24 * 2**20
         ),
-    )(pair, token_mask, w_in.transpose(1, 2, 0), w_gate.T, w_out, cotangent)
+    )(*args)
     return out[0], out[1]
 
 
@@ -421,6 +483,7 @@
     rows, cols, chans = pair.shape
     n = token_mask.shape[0]
     small = n <= 32 and n % 8 == 0 and rows % 2 == 0 and cols % 4 == 0 and rows * n % 16 == 0
+    small = small and cols % rows == 0
     shaped = n_col == 2 and n_chan == 2 and chans == 64 and w_in.shape == (128, 4, 64)
     if small and shaped and -(-cols // 16) * 16 - cols <= 8:
         return gathered(n_row, pair, token_mask, w_in, w_gate, w_out, cotangent)

time: 17.7 us -> 16.1 us (0.910)
  Pallas kernels: 15.5 us -> 14.6 us
  local copies, waits for them, and re-layouts: 1.38 us -> 0.62 us
    pallas_call x1, Pallas kernels: 15.5 us -> 14.6 us  [gathered(): pl.pallas_call(functools.partial(kernel, n_row), out_shape=pltpu.VMEM((2,...]
    squeeze x1, local copies, waits for them, and re-layouts: 1.38 us -> 0.62 us  [gathered(): return (out[0], out[1])]
where the time goes in v3:
time: 16.1 us; the launch traced here: 15.9 us
  Pallas kernels  14.6 us (91%)
  between operations  0.64 us (4%)
  local copies, waits for them, and re-layouts  0.62 us (4%)
    pallas_call x1, Pallas kernels, gathered(): pl.pallas_call(functools.partial(kernel, n_row), out_shape=pltpu.VMEM((2,...  14.6 us
    squeeze x1, local copies, waits for them, and re-layouts, gathered(): return (out[0], out[1])  0.62 us

profile of v3, /device:TPU:0, one launch (start us, length us, event | category | flops | bytes accessed | tf_op | source)
XLA Modules:
  0.0 15.9 jit_solution(9937560965689894339)
XLA Ops:
  0.6 14.6 %shard_map.77 = bf16[2,6,12,64]{3,2,1,0:T(8,128)(2,1)S(1)} custom-call(bf16[6,12,64]{2,1,0:T(8,128)(2,1)} %pair_hbm.1, s32[24]{0:T(128)} %mask_hbm.1, bf16[4,64,128]{2,1,0:T(8,128)(2,1)} %bitcast.6, bf16[64,128]{1,0:T(8,128)(2,1)} %bitcast.7, bf16[64,128]{1,0:T(8,128)(2,1)} %w_out_hbm.1, bf16[6,12,64]{2,1,0:T(8,128)(2,1)} %cot_hbm.1), custom_call_target="tpu_custom_call" | custom-call | tf_op jit(solution)/shard_map/pallas_call | solution.py:353
  15.3 0.6 %slice_bitcast_fusion = (bf16[6,12,64]{2,1,0:T(8,128)(2,1)}, bf16[6,12,64]{2,1,0:T(8,128)(2,1)}) fusion(bf16[2,6,12,64]{3,2,1,0:T(8,128)(2,1)S(1)} %shard_map.77), kind=kLoop, calls=%fused_computation | loop fusion | bytes 36864 | tf_op jit(solution)/shard_map/squeeze | solution.py:372

commit v4 on v3

--- a/solution.py
+++ b/solution.py
@@ -43,19 +43,21 @@
 
 def kernel(
     n_row, pair_hbm, mask_hbm, w_in_hbm, w_gate_hbm, w_out_hbm, cot_hbm, out_ref,
-    pair_ref, cot_ref, mask_ref, in_sem, pbuf, cbuf, wbuf, z_s, zh_s, c_s, l_s, r_s, mj_s, u_s, dg_s, da_s, db_s,
-    p_send, p_fwd, p_recv, c_send, c_fwd, c_recv, w_send, w_recv,
+    pair_ref, cot_ref, mask_ref, in_sem, pbuf, cbuf, obuf, wbuf, pp_s, cp_s, z_s, zh_s, ca_s, cb_s, l_s, r_s, mj_s, u_s, dg_s, da_s, db_s,
+    p_send, p_recv, p_fwd, p_near, c_send, c_recv, c_fwd, c_near, w_send, w_recv,
 ):
     f32, bf16 = jnp.float32, jnp.bfloat16
     rows, cols, _ = pair_ref.shape
     n = rows * n_row
     width = 2 * pair_ref.shape[2]
     half_rows = rows // 2
-    pad = pbuf.shape[4]
+    pad = -(-cols // 16) * 16
+    pieces = cols // rows
     block = rows * n
     r, c, h = lax.axis_index("row"), lax.axis_index("col"), lax.axis_index("chan")
     other_c, other_h = 1 - c, 1 - h
     wanted_c = lax.div(r * rows, cols)
+    wanted_piece = r - wanted_c * (cols // rows)
     plane = [(0, 1), (1, 0), (1, 1)]
 
     def partner(dc, dh):
@@ -93,91 +95,79 @@
         device = {"row": lax.rem(r + dr, n_row), "col": pc, "chan": ph}
         pl.semaphore_signal(barrier, inc=1, device_id=device, device_id_type=MESH)
 
-    def pack(ref, buf):
+    def packed(ref):
         x = ref[...].astype(f32)
-        x = jnp.concatenate([x[:half_rows], x[half_rows:]], axis=-1)
-        buf[r, c, h] = jnp.zeros(buf.shape[3:], bf16)
-        buf[r, c, h, :, 0:cols, :] = x.astype(bf16)
+        return jnp.concatenate([x[:half_rows], x[half_rows:]], axis=-1)
+
+    def pack_pair():
+        x = packed(pair_ref)
+        for t in range(half_rows):
+            pp_s[t * cols : (t + 1) * cols, :] = x[t]
+        pbuf[r, c, h] = pp_s[...].astype(bf16)
+
+    def pack_cot():
+        x = packed(cot_ref)
+        for piece in range(pieces):
+            for t in range(half_rows):
+                cp_s[piece, t * rows : (t + 1) * rows, :] = x[t, piece * rows : (piece + 1) * rows]
+            cbuf[r, c, h, piece] = cp_s[piece].astype(bf16)
 
     loads[0].wait()
-    pack(pair_ref, pbuf)
-    pl.semaphore_wait(barrier, len(everyone))
+    pack_pair()
 
     def far_copy(buf, slot, send, recv, device):
+        part = buf.at[slot] if slot else buf
         return pltpu.make_async_remote_copy(
-            src_ref=buf.at[slot], dst_ref=buf.at[slot], send_sem=send, recv_sem=recv,
+            src_ref=part, dst_ref=part, send_sem=send, recv_sem=recv,
             device_id=device, device_id_type=MESH,
         )
 
-    def spread(buf, send, fwd, recv):
-        sent = []
-        own = (r, c, h)
-        for dr, dh in far:
-            pr, ph = place(dr, dh)
-            sent.append(
-                far_copy(buf, own, send.at[dr, dh], recv.at[own], {"row": pr, "chan": ph})
-            )
-        sent.append(far_copy(buf, own, fwd.at[0, 0], recv.at[own], {"col": other_c}))
-        for copy in sent:
-            copy.start()
-        return sent
-
-    def relay(buf, fwd, recv, dr):
+    def shard_copy(dr, dh):
+        pr, ph = place(dr, dh)
+        return far_copy(pbuf, (r, c, h), p_send.at[dr, dh], p_recv.at[r, h], {"row": pr, "chan": ph})
+
+    def relay(dr):
+        pr = lax.rem(r + dr, n_row)
         for dh in range(2):
-            if (dr, dh) == (0, 0):
-                continue
-            pr, ph = place(dr, dh)
-            slot = (pr, c, ph)
-            copy = far_copy(buf, slot, fwd.at[dr, dh], recv.at[slot], {"col": other_c})
-            copy.wait_recv()
-            copy.start()
-            sent.append(copy)
-
-    def wait_for(buf, recv, slot):
-        far_copy(buf, slot, w_send.at[0], recv.at[slot], {"col": other_c}).wait_recv()
+            if (dr, dh) != (0, 0):
+                ph = lax.rem(h + dh, 2)
+                far_copy(pbuf, (pr, c, ph), p_send.at[dr, dh], p_recv.at[pr, ph], {"chan": ph}).wait_recv()
+        return far_copy(pbuf, (pr, c), p_fwd.at[dr], p_near.at[dr], {"col": other_c})
 
     def cot_copies(act):
-        own = (r, c, h)
-        for dr in range(n_row):
+        act(far_copy(cbuf, (r, c, h), c_send.at[0, 1], c_recv.at[r, h], {"chan": other_h}))
+        for dr in range(1, n_row):
             pr = lax.rem(r + dr, n_row)
 
-            def to_plane():
-                for dc, dh in [(0, 0), (0, 1)] if dr else [(0, 1), (1, 0)]:
-                    pc, ph = partner(dc, dh)
-                    device = {"row": pr, "col": pc, "chan": ph}
-                    act(far_copy(cbuf, own, c_send.at[dr, dc, dh], c_recv.at[own], device))
-
-            if dr:
-                pl.when(lax.div(pr * rows, cols) == c)(to_plane)
-            else:
-                to_plane()
-
-    def cot_relay(act):
-        def pass_on(dr, dh):
-            slot = (lax.rem(r + dr, n_row), c, lax.rem(h + dh, 2))
-            act(far_copy(cbuf, slot, c_fwd.at[dr, dh], c_recv.at[slot], {"col": other_c}))
-
-        pass_on(0, 1)
+            def to_row():
+                for dh in range(2):
+                    act(pltpu.make_async_remote_copy(
+                        src_ref=cbuf.at[r, c, h, pr - c * pieces], dst_ref=obuf.at[r, h],
+                        send_sem=c_send.at[dr, dh], recv_sem=c_recv.at[r, h],
+                        device_id={"row": pr, "chan": lax.rem(h + dh, 2)}, device_id_type=MESH,
+                    ))
+
+            pl.when(lax.div(pr * rows, cols) == c)(to_row)
+
+    def cot_relay(act, arrive):
+        if arrive:
+            far_copy(cbuf, (r, c, other_h), c_send.at[0, 1], c_recv.at[r, other_h], {"chan": other_h}).wait_recv()
+        act(far_copy(cbuf, (r, c), c_fwd.at[0], c_near.at[0], {"col": other_c}))
 
         @pl.when(c == wanted_c)
         def _():
-            for dr in range(1, n_row):
-                for dh in range(2):
-                    pass_on(dr, dh)
-
-    sent = spread(pbuf, p_send, p_fwd, p_recv)
-    for load in loads[1:5]:
-        load.wait()
-
-    def weights(core, rows):
-        return (pl.ds(3 * core, 3), rows)
-
-    theirs = pl.ds(pl.multiple_of(other_h * (width // 2), width // 2), width // 2)
-    w_far = far_copy(wbuf, weights(c, mine), w_send.at[0], w_recv.at[0], {"chan": other_h})
-    w_far.start()
+            if arrive:
+                for dr in range(1, n_row):
+                    pr = lax.rem(r + dr, n_row)
+                    for ph in range(2):
+                        far_copy(obuf, (pr, ph), c_send.at[0, 1], c_recv.at[pr, ph], {"chan": other_h}).wait_recv()
+            act(far_copy(obuf, (), c_fwd.at[1], c_near.at[1], {"col": other_c}))
+
+    def start(copy):
+        copy.start()
+
     loads[5].wait()
-    pack(cot_ref, cbuf)
-    cot_copies(lambda copy: copy.start())
+    pack_cot()
 
     loads[6].wait()
     token = lax.broadcasted_iota(jnp.int32, (n, width), 0)
@@ -189,51 +179,62 @@
     tail = z_s.shape[0] - n * n
     for s in (z_s, zh_s, l_s, r_s):
         s[n * n : n * n + tail, :] = jnp.zeros((tail, width), f32)
-
-    relay(pbuf, p_fwd, p_recv, 0)
+    obuf[r] = jnp.zeros(obuf.shape[1:], bf16)
+    for load in loads[1:5]:
+        load.wait()
+    pl.semaphore_wait(barrier, len(everyone))
+    sent = [shard_copy(dr, dh) for dr, dh in far]
+    for copy in sent:
+        copy.start()
+
+    def weights(core, rows):
+        return (pl.ds(3 * core, 3), rows)
+
+    theirs = pl.ds(pl.multiple_of(other_h * (width // 2), width // 2), width // 2)
+    w_far = far_copy(wbuf, weights(c, mine), w_send.at[0], w_recv.at[0], {"chan": other_h})
+    w_far.start()
+    cot_copies(start)
+    sent.append(relay(0))
+    sent[-1].start()
     w_near = far_copy(wbuf, weights(c, theirs), w_send.at[1], w_recv.at[1], {"col": other_c})
     far_copy(wbuf, weights(c, theirs), w_send.at[0], w_recv.at[0], {"chan": other_h}).wait_recv()
     w_near.start()
     sent += [w_far, w_near]
     for dr in range(1, n_row):
-        relay(pbuf, p_fwd, p_recv, dr)
+        sent.append(relay(dr))
+        sent[-1].start()
     far_copy(wbuf, weights(other_c, theirs), w_send.at[1], w_recv.at[1], {"col": other_c}).wait_recv()
 
     w_left = wbuf[0:2].reshape(2 * width, width)
     w_right = wbuf[3:5].reshape(2 * width, width)
     w_gate, w_out = wbuf[2], wbuf[5]
 
-    def unpack(buf, dst, br, bc):
-        for part, full in enumerate(merge(buf[br, bc, 0], buf[br, bc, 1])):
+    def unpack_pair(br, bc):
+        for part, full in enumerate(merge(pbuf[br, bc, 0], pbuf[br, bc, 1])):
             for t in range(half_rows):
                 first = pl.multiple_of(br * block, 8) + (part * half_rows + t) * n + bc * cols
-                dst[pl.ds(first, cols), :] = full[t, 0:cols, :]
+                z_s[pl.ds(first, cols), :] = full[t * cols : (t + 1) * cols]
 
     for dr in range(n_row):
-        br = lax.rem(r + dr, n_row)
-        for dh in range(2):
-            wait_for(pbuf, p_recv, (br, other_c, lax.rem(h + dh, 2)))
+        slot = (lax.rem(r + dr, n_row), other_c)
+        far_copy(pbuf, slot, p_fwd.at[dr], p_near.at[dr], {"col": other_c}).wait_recv()
+    for br in range(n_row):
         for bc in range(2):
-            unpack(pbuf, z_s, br, bc)
-        at = pl.ds(pl.multiple_of(br * block, 8), block)
-        z = z_s[at, :]
-        mean, rstd = norm_stats(z)
-        zh = (z - mean) * rstd
-        zh_s[at, :] = zh
-        zn = zh.astype(bf16)
-        pm = jnp.concatenate([mj * mask_ref[br * rows + t].astype(f32) for t in range(rows)], axis=0)
-        proj = dot(zn, w_left, True)
-        left = pm * sigmoid(proj[:, width:]) * proj[:, :width]
-        l_s[at, :] = left.astype(bf16).astype(f32)
-        proj = dot(zn, w_right, True)
-        right = pm * sigmoid(proj[:, width:]) * proj[:, :width]
-        r_s[at, :] = right.astype(bf16).astype(f32)
-
-    def received_and_passed(copy):
-        copy.wait_recv()
-        copy.start()
-
-    cot_relay(received_and_passed)
+            unpack_pair(br, bc)
+    z = z_s[0 : n * n, :]
+    mean, rstd = norm_stats(z)
+    zh = (z - mean) * rstd
+    zh_s[0 : n * n, :] = zh
+    zn = zh.astype(bf16)
+    for w, dst in ((w_left, l_s), (w_right, r_s)):
+        proj = dot(zn, w, True)
+        gated = sigmoid(proj[:, width:]) * proj[:, :width]
+        for i in range(n):
+            at = slice(i * n, (i + 1) * n)
+            pm = mj * mask_ref[i].astype(f32)
+            dst[at, :] = (pm * gated[at]).astype(bf16).astype(f32)
+
+    cot_relay(start, True)
 
     def products(step, start):
         sums = lax.fori_loop(0, n, step, ((start,) * rows,) * 2, unroll=24)
@@ -300,21 +301,31 @@
 
     put(0, own_cells(u_s, 0))
 
-    for bh in range(2):
-        wait_for(cbuf, c_recv, (r, other_c, bh))
+    far_copy(cbuf, (r, other_c), c_fwd.at[0], c_near.at[0], {"col": other_c}).wait_recv()
+
+    @pl.when(c != wanted_c)
+    def _():
+        far_copy(obuf, (), c_fwd.at[1], c_near.at[1], {"col": other_c}).wait_recv()
+
     for bc in range(2):
-        unpack(cbuf, c_s, r, bc)
-    for dr in range(1, n_row):
-        br = lax.rem(r + dr, n_row)
-        for bh in range(2):
-            slot = (br, wanted_c, bh)
-            pl.when(c != wanted_c)(functools.partial(wait_for, cbuf, c_recv, slot))
-        unpack(cbuf, c_s, br, wanted_c)
-
-    cot_a = c_s[own_rows, :]
+        for piece in range(pieces):
+            for part, full in enumerate(merge(cbuf[r, bc, 0, piece], cbuf[r, bc, 1, piece])):
+                for t in range(half_rows):
+                    first = (part * half_rows + t) * n + bc * cols + piece * rows
+                    ca_s[first : first + rows, :] = full[t * rows : (t + 1) * rows]
+    for br in range(n_row):
+        theirs = [
+            jnp.where(br == r, cbuf[r, wanted_c, bh, wanted_piece].astype(f32), obuf[br, bh].astype(f32))
+            for bh in range(2)
+        ]
+        for part, full in enumerate(merge(*theirs)):
+            first = (br * rows + part * half_rows) * rows
+            cb_s[first : first + half_rows * rows, :] = full
+    cot_a = ca_s[...]
+    cot_b = jnp.concatenate([cb_s[pl.ds(j, n, stride=rows), :] for j in range(rows)], axis=0)
     dg_s[0:block, :] = cot_a * proj_out * gate_a * (1.0 - gate_a)
     da_s[...] = backward(xhat_a, rstd_a, gate_a, cot_a)
-    db_s[...] = backward(xhat_b, rstd_b, gate_b, turned_block(c_s))
+    db_s[...] = backward(xhat_b, rstd_b, gate_b, cot_b)
 
     def gradient_step(j, sums):
         out = []
@@ -332,8 +343,11 @@
     put(1, (dzn - lane_mean(dzn) - zhat * lane_mean(dzn * zhat)) * rstd)
     for copy in sent:
         copy.wait_send()
-    cot_copies(lambda copy: copy.wait_send())
-    cot_relay(lambda copy: copy.wait_send())
+    def finish(copy):
+        copy.wait_send()
+
+    cot_copies(finish)
+    cot_relay(finish, False)
 
 
 def gathered(n_row, pair, token_mask, w_in, w_gate, w_out, cotangent):
@@ -341,9 +355,10 @@
     rows, cols, chans = pair.shape
     n = rows * n_row
     width = 2 * chans
-    pad = -(-cols // 16) * 16
     vmem = pl.BlockSpec(memory_space=pltpu.VMEM)
-    shards = pltpu.VMEM((n_row, 2, 2, rows // 2, pad, width), bf16)
+    pair_shard, cot_shard = (rows // 2 * cols, width), (cols // rows, rows // 2 * rows, width)
+    pair_shards = pltpu.VMEM((n_row, 2, 2) + pair_shard, bf16)
+    cot_shards = pltpu.VMEM((n_row, 2, 2) + cot_shard, bf16)
     cells = pltpu.VMEM((n * n + 8, width), f32)
     block = pltpu.VMEM((rows * n, width), f32)
     block_and_tail = pltpu.VMEM((rows * n + 8, width), f32)
@@ -358,11 +373,12 @@
         scratch_shapes=[
             pltpu.VMEM(pair.shape, bf16), pltpu.VMEM(pair.shape, bf16),
             pltpu.SMEM(token_mask.shape, jnp.int32), dma((7,)),
-            shards, shards, pltpu.VMEM((6, width, width), bf16),
-            cells, cells, cells, cells, cells, pltpu.VMEM((n + 8, width), f32),
+            pair_shards, cot_shards, pltpu.VMEM((n_row, 2) + cot_shard[1:], bf16), pltpu.VMEM((6, width, width), bf16),
+            pltpu.VMEM(pair_shard, f32), pltpu.VMEM(cot_shard, f32),
+            cells, cells, block, block, cells, cells, pltpu.VMEM((n + 8, width), f32),
             block_and_tail, block_and_tail, block, block,
-            dma((n_row, 2)), dma((n_row, 2)), dma((n_row, 2, 2)),
-            dma((n_row, 2, 2)), dma((n_row, 2)), dma((n_row, 2, 2)),
+            dma((n_row, 2)), dma((n_row, 2)), dma((n_row,)), dma((n_row,)),
+            dma((n_row, 2)), dma((n_row, 2)), dma((2,)), dma((2,)),
             dma((2,)), dma((2,)),
         ],
         compiler_params=pltpu.CompilerParams(

time: 16.1 us -> 14.9 us (0.925)
  Pallas kernels: 14.6 us -> 13.4 us
    pallas_call x1, Pallas kernels: 14.6 us -> 13.4 us  [gathered(): pl.pallas_call(functools.partial(kernel, n_row), out_shape=pltpu.VMEM((2,...]
where the time goes in v4:
time: 14.9 us; the launch traced here: 14.7 us
  Pallas kernels  13.4 us (90%)
  between operations  0.64 us (4%)
  local copies, waits for them, and re-layouts  0.62 us (4%)
    pallas_call x1, Pallas kernels, gathered(): pl.pallas_call(functools.partial(kernel, n_row), out_shape=pltpu.VMEM((2,...  13.4 us
    squeeze x1, local copies, waits for them, and re-layouts, gathered(): return (out[0], out[1])  0.62 us

profile of v4, /device:TPU:0, one launch (start us, length us, event | category | flops | bytes accessed | tf_op | source)
XLA Modules:
  0.0 14.7 jit_solution(3059700818506734169)
XLA Ops:
  0.6 13.4 %shard_map.77 = bf16[2,6,12,64]{3,2,1,0:T(8,128)(2,1)S(1)} custom-call(bf16[6,12,64]{2,1,0:T(8,128)(2,1)} %pair_hbm.1, s32[24]{0:T(128)} %mask_hbm.1, bf16[4,64,128]{2,1,0:T(8,128)(2,1)} %bitcast.6, bf16[64,128]{1,0:T(8,128)(2,1)} %bitcast.7, bf16[64,128]{1,0:T(8,128)(2,1)} %w_out_hbm.1, bf16[6,12,64]{2,1,0:T(8,128)(2,1)} %cot_hbm.1), custom_call_target="tpu_custom_call" | custom-call | tf_op jit(solution)/shard_map/pallas_call | solution.py:368
  14.1 0.6 %slice_bitcast_fusion = (bf16[6,12,64]{2,1,0:T(8,128)(2,1)}, bf16[6,12,64]{2,1,0:T(8,128)(2,1)}) fusion(bf16[2,6,12,64]{3,2,1,0:T(8,128)(2,1)S(1)} %shard_map.77), kind=kLoop, calls=%fused_computation | loop fusion | bytes 36864 | tf_op jit(solution)/shard_map/squeeze | solution.py:388

commit v5 on v4

--- a/solution.py
+++ b/solution.py
@@ -43,7 +43,7 @@
 
 def kernel(
     n_row, pair_hbm, mask_hbm, w_in_hbm, w_gate_hbm, w_out_hbm, cot_hbm, out_ref,
-    pair_ref, cot_ref, mask_ref, in_sem, pbuf, cbuf, obuf, wbuf, pp_s, cp_s, z_s, zh_s, ca_s, cb_s, l_s, r_s, mj_s, u_s, dg_s, da_s, db_s,
+    pair_ref, cot_ref, mask_ref, in_sem, pbuf, cbuf, obuf, wbuf, pp_s, cp_s, z_s, zh_s, ca_s, cb_s, zd_s, pm_s, l_s, r_s, mj_s, u_s, dg_s, da_s, db_s,
     p_send, p_recv, p_fwd, p_near, c_send, c_recv, c_fwd, c_near, w_send, w_recv,
 ):
     f32, bf16 = jnp.float32, jnp.bfloat16
@@ -176,6 +176,10 @@
         mj = jnp.where(token == j, mask_ref[j].astype(f32), mj)
     mj_s[...] = jnp.zeros(mj_s.shape, f32)
     mj_s[0:n, :] = mj
+    for bc in range(2):
+        for i in range(n):
+            pm = mj[bc * cols : (bc + 1) * cols] * mask_ref[i].astype(f32)
+            pm_s[bc, i * cols : (i + 1) * cols, :] = pm
     tail = z_s.shape[0] - n * n
     for s in (z_s, zh_s, l_s, r_s):
         s[n * n : n * n + tail, :] = jnp.zeros((tail, width), f32)
@@ -183,9 +187,10 @@
     for load in loads[1:5]:
         load.wait()
     pl.semaphore_wait(barrier, len(everyone))
-    sent = [shard_copy(dr, dh) for dr, dh in far]
-    for copy in sent:
+    direct = [shard_copy(dr, dh) for dr, dh in far]
+    for copy in direct:
         copy.start()
+    sent = []
 
     def weights(core, rows):
         return (pl.ds(3 * core, 3), rows)
@@ -199,10 +204,12 @@
     w_near = far_copy(wbuf, weights(c, theirs), w_send.at[1], w_recv.at[1], {"col": other_c})
     far_copy(wbuf, weights(c, theirs), w_send.at[0], w_recv.at[0], {"chan": other_h}).wait_recv()
     w_near.start()
-    sent += [w_far, w_near]
+    sent.append(w_near)
     for dr in range(1, n_row):
         sent.append(relay(dr))
         sent[-1].start()
+    for copy in direct + [w_far]:
+        copy.wait_send()
     far_copy(wbuf, weights(other_c, theirs), w_send.at[1], w_recv.at[1], {"col": other_c}).wait_recv()
 
     w_left = wbuf[0:2].reshape(2 * width, width)
@@ -215,26 +222,33 @@
                 first = pl.multiple_of(br * block, 8) + (part * half_rows + t) * n + bc * cols
                 z_s[pl.ds(first, cols), :] = full[t * cols : (t + 1) * cols]
 
+    def project(bc):
+        for br in range(n_row):
+            for part, full in enumerate(merge(pbuf[br, bc, 0], pbuf[br, bc, 1])):
+                first = (br * rows + part * half_rows) * cols
+                zd_s[first : first + half_rows * cols, :] = full
+        z = zd_s[...]
+        mean, rstd = norm_stats(z)
+        zh = (z - mean) * rstd
+        zn = zh.astype(bf16)
+        pm = pm_s[bc]
+        results = [(z_s, z), (zh_s, zh)]
+        for w, dst in ((w_left, l_s), (w_right, r_s)):
+            proj = dot(zn, w, True)
+            value = pm * sigmoid(proj[:, width:]) * proj[:, :width]
+            results.append((dst, value.astype(bf16).astype(f32)))
+        for dst, value in results:
+            zd_s[...] = value
+            for i in range(n):
+                dst[pl.ds(i * n + bc * cols, cols), :] = zd_s[i * cols : (i + 1) * cols, :]
+
+    project(c)
     for dr in range(n_row):
         slot = (lax.rem(r + dr, n_row), other_c)
         far_copy(pbuf, slot, p_fwd.at[dr], p_near.at[dr], {"col": other_c}).wait_recv()
-    for br in range(n_row):
-        for bc in range(2):
-            unpack_pair(br, bc)
-    z = z_s[0 : n * n, :]
-    mean, rstd = norm_stats(z)
-    zh = (z - mean) * rstd
-    zh_s[0 : n * n, :] = zh
-    zn = zh.astype(bf16)
-    for w, dst in ((w_left, l_s), (w_right, r_s)):
-        proj = dot(zn, w, True)
-        gated = sigmoid(proj[:, width:]) * proj[:, :width]
-        for i in range(n):
-            at = slice(i * n, (i + 1) * n)
-            pm = mj * mask_ref[i].astype(f32)
-            dst[at, :] = (pm * gated[at]).astype(bf16).astype(f32)
-
     cot_relay(start, True)
+    project(other_c)
+
 
     def products(step, start):
         sums = lax.fori_loop(0, n, step, ((start,) * rows,) * 2, unroll=24)
@@ -375,7 +389,7 @@
             pltpu.SMEM(token_mask.shape, jnp.int32), dma((7,)),
             pair_shards, cot_shards, pltpu.VMEM((n_row, 2) + cot_shard[1:], bf16), pltpu.VMEM((6, width, width), bf16),
             pltpu.VMEM(pair_shard, f32), pltpu.VMEM(cot_shard, f32),
-            cells, cells, block, block, cells, cells, pltpu.VMEM((n + 8, width), f32),
+            cells, cells, block, block, pltpu.VMEM((n * cols, width), f32), pltpu.VMEM((2, n * cols, width), f32), cells, cells, pltpu.VMEM((n + 8, width), f32),
             block_and_tail, block_and_tail, block, block,
             dma((n_row, 2)), dma((n_row, 2)), dma((n_row,)), dma((n_row,)),
             dma((n_row, 2)), dma((n_row, 2)), dma((2,)), dma((2,)),

time: 14.9 us -> 14.5 us (0.973)
  Pallas kernels: 13.4 us -> 13.1 us
    pallas_call x1, Pallas kernels: 13.4 us -> 13.1 us  [gathered(): pl.pallas_call(functools.partial(kernel, n_row), out_shape=pltpu.VMEM((2,...]
where the time goes in v5:
time: 14.5 us; the launch traced here: 14.3 us
  Pallas kernels  13.1 us (90%)
  between operations  0.64 us (4%)
  local copies, waits for them, and re-layouts  0.62 us (4%)
    pallas_call x1, Pallas kernels, gathered(): pl.pallas_call(functools.partial(kernel, n_row), out_shape=pltpu.VMEM((2,...  13.1 us
    squeeze x1, local copies, waits for them, and re-layouts, gathered(): return (out[0], out[1])  0.62 us

profile of v5, /device:TPU:0, one launch (start us, length us, event | category | flops | bytes accessed | tf_op | source)
XLA Modules:
  0.0 14.3 jit_solution(13242708974398926413)
XLA Ops:
  0.6 13.1 %shard_map.77 = bf16[2,6,12,64]{3,2,1,0:T(8,128)(2,1)S(1)} custom-call(bf16[6,12,64]{2,1,0:T(8,128)(2,1)} %pair_hbm.1, s32[24]{0:T(128)} %mask_hbm.1, bf16[4,64,128]{2,1,0:T(8,128)(2,1)} %bitcast.6, bf16[64,128]{1,0:T(8,128)(2,1)} %bitcast.7, bf16[64,128]{1,0:T(8,128)(2,1)} %w_out_hbm.1, bf16[6,12,64]{2,1,0:T(8,128)(2,1)} %cot_hbm.1), custom_call_target="tpu_custom_call" | custom-call | tf_op jit(solution)/shard_map/pallas_call | solution.py:382
  13.7 0.6 %slice_bitcast_fusion = (bf16[6,12,64]{2,1,0:T(8,128)(2,1)}, bf16[6,12,64]{2,1,0:T(8,128)(2,1)}) fusion(bf16[2,6,12,64]{3,2,1,0:T(8,128)(2,1)S(1)} %shard_map.77), kind=kLoop, calls=%fused_computation | loop fusion | bytes 36864 | tf_op jit(solution)/shard_map/squeeze | solution.py:402
